TPU v7x, 32 devices: a whole 2x2x4 slice. The times are simulated.
32 devices in a mesh: tok: 4 (over x, core), voc: 8 (over z, y).
Axes of the slice: x: 2, y: 2, z: 4, core: 2. Of those that a mesh axis runs over, the one named last changes fastest.
Arguments:
- hidden: bfloat16 [64, 32, 2048], P(('tok', 'voc')), may hold values from -40 to 40
- norm_gain: float32 [2048], replicated, may hold values from 0.5 to 1.5
- head_weight: bfloat16 [2048, 51200], P(None, 'voc'), may hold values from -2 to 2
- lengths: int32 [64], P(('tok', 'voc')), may hold values from 12 to 24, as said below
- offsets: int32 [64], P(('tok', 'voc')), may hold values from 0 to 8
- slot_request: int32 [64], replicated, may hold values from 0 to 63, each once
- targets: int32 [64, 32], P(('tok', 'voc')), may hold values from 0 to 51199
Outputs:
- token_logprob: float32 [64, 32], P(('tok', 'voc'))
- token_entropy: float32 [64, 32], P(('tok', 'voc'))
Inputs may be any that keep to these rules, and one draw needn't show every extreme that they name: `lengths`: each request has 12 to 24 response rows; all 2 requests of some one scoring device have exactly 24. Response rows end within the window: offsets + lengths <= 32. `slot_request`: every request appears in exactly one slot.
All inputs are finite; a program needn't handle non-finite values.
Results may differ from a plain program's by a relative error of at most 0.00145.
Values may be sent and summed in bfloat16 or wider, within the bound.
No kernel may reach another device: no remote copies, remote signals or barrier semaphores. Data moves between devices by JAX's collectives and lax.ppermute only.
A program may use at most 128 MiB of HBM per device.

v0:
```python
import jax
import jax.numpy as jnp
from jax import lax
from jax.sharding import PartitionSpec as P

EPS = 1e-06


def normalize(hidden, norm_gain):
    values = hidden.astype(jnp.float32)
    square = jnp.mean(values * values, axis=-1, keepdims=True)
    return (values * lax.rsqrt(square + EPS) * norm_gain).astype(jnp.bfloat16)


def shards(hidden, norm_gain, head_weight, lengths, offsets, slot_request, targets):
    req_dev, span, width = hidden.shape
    vocab_dev = head_weight.shape[1]
    normed = normalize(hidden, norm_gain).reshape(req_dev * span, width)
    position = jnp.arange(span, dtype=jnp.int32)[None, :]
    in_span = (
        (position >= offsets[:, None]) & (position < offsets[:, None] + lengths[:, None])
    ).reshape(-1)
    flat_targets = targets.reshape(-1)
    own_count = normed.shape[0]
    group_matrix, group_targets = (
        lax.all_gather(normed, "voc", axis=0, tiled=True),
        lax.all_gather(flat_targets, "voc", axis=0, tiled=True),
    )
    logits = jnp.dot(group_matrix, head_weight, preferred_element_type=jnp.float32)
    shard_index = lax.axis_index("voc")
    local_column = group_targets - shard_index * vocab_dev
    target_hit = jnp.arange(vocab_dev, dtype=jnp.int32)[None, :] == local_column[:, None]
    picked = jnp.sum(jnp.where(target_hit, logits, 0.0), axis=1)
    row_peak = jnp.max(logits, axis=1)
    scaled = jnp.exp(logits - row_peak[:, None])
    exp_sum = jnp.sum(scaled, axis=1)
    exp_dot = jnp.sum(scaled * logits, axis=1)
    first_row = shard_index * own_count
    peak_all = lax.pmax(row_peak, "voc")
    rescale = jnp.exp(row_peak - peak_all)
    sum_all, dot_all, pick_all = lax.psum((exp_sum * rescale, exp_dot * rescale, picked), "voc")
    peak_own = lax.dynamic_slice_in_dim(peak_all, first_row, own_count)
    sum_own = lax.dynamic_slice_in_dim(sum_all, first_row, own_count)
    dot_own = lax.dynamic_slice_in_dim(dot_all, first_row, own_count)
    pick_own = lax.dynamic_slice_in_dim(pick_all, first_row, own_count)
    log_total = jnp.log(sum_own)
    logprob = pick_own - peak_own - log_total
    entropy = peak_own + log_total - dot_own / sum_own
    logprob_rows = jnp.where(in_span, logprob, 0.0).reshape(req_dev, span)
    entropy_rows = jnp.where(in_span, entropy, 0.0).reshape(req_dev, span)
    device = lax.axis_index(("tok", "voc"))
    every_logprob, every_entropy = (
        lax.all_gather(logprob_rows, ("tok", "voc"), axis=0, tiled=True),
        lax.all_gather(entropy_rows, ("tok", "voc"), axis=0, tiled=True),
    )
    wanted = device * req_dev + jnp.arange(req_dev, dtype=jnp.int32)
    picking = slot_request[None, :] == wanted[:, None]
    token_logprob = jnp.sum(jnp.where(picking[:, :, None], every_logprob[None, :, :], 0.0), axis=1)
    token_entropy = jnp.sum(jnp.where(picking[:, :, None], every_entropy[None, :, :], 0.0), axis=1)
    return (token_logprob, token_entropy)


def solution(mesh):
    placed = (
        P(("tok", "voc"), None, None),
        P(),
        P(None, "voc"),
        P(("tok", "voc")),
        P(("tok", "voc")),
        P(),
        P(("tok", "voc"), None),
    )
    return jax.shard_map(
        shards,
        mesh=mesh,
        in_specs=placed,
        out_specs=(P(("tok", "voc"), None), P(("tok", "voc"), None)),
        check_vma=False,
    )
```

profile of v0, /device:TPU:0, one launch (start us, length us, event | category | flops | bytes accessed | tf_op | source)
XLA Modules:
  0.0 266.0 jit_solution(7772214468000146201)
XLA Ops:
  7.2 0.0 all-gather.4.cloned.1.call-start
  7.2 1.1 fusion.1
  8.3 1.8 fusion.3
  10.1 0.0 all-gather.4.cloned.1.call-update
  10.1 0.7 add.46
  10.8 0.7 compare_and_fusion
  11.5 0.1 and.10
  11.6 0.8 reshape.74
  12.4 1.2 dynamic-slice
  14.3 0.2 dynamic-update-slice
  14.5 13.2 %all-reduce = s32[512]{0:T(512)S(1)} all-reduce(s32[512]{0:T(512)S(1)} %dynamic-update-slice), channel_id=1, replica_groups=mesh['tok'=4,'voc'=8] {'voc'}, use_global_device_ids=true, to_apply=%add | all-reduce | flops 512 | bytes 4096
  27.7 0.7 broadcast_compare_fusion
  28.4 34.0 %all-gather.4.cloned.1.call-done = bf16[512,2048]{1,0:T(8,128)(2,1)} async-done(((bf16[64,2048]{1,0:T(8,128)(2,1)}), bf16[512,2048]{1,0:T(8,128)(2,1)}) %all-gather.4.cloned.1.call-update) | async-done | bytes 2097168 | tf_op jit(solution)/shard_map/all_gather | solution.py:26
  62.4 22.5 %fusion.6 = (f32[512]{0:T(512)S(1)}, f32[512,6400]{1,0:T(8,128)}) fusion(bf16[512,2048]{1,0:T(8,128)(2,1)} %all-gather.4.cloned.1.call-done, bf16[2048,6400]{1,0:T(8,128)(2,1)} %param.9), kind=kOutput, calls=%fused_computation.22 | convolution fusion | flops 13425049600 | bytes 41420800 | tf_op jit(solution)/shard_map/dot_general | solution.py:29
  85.0 18.9 %pmax.7 = f32[512]{0:T(512)S(1)} all-reduce(f32[512]{0:T(512)S(1)} %get-tuple-element.14), channel_id=1, replica_groups=mesh['tok'=4,'voc'=8] {'voc'}, use_global_device_ids=true, to_apply=%region_4.5 | all-reduce | flops 512 | bytes 4096 | tf_op jit(solution)/shard_map/pmax | solution.py:39
  103.9 7.6 %multiply_reduce_fusion = (f32[512]{0:T(512)S(1)}, f32[512]{0:T(512)S(1)}, f32[512]{0:T(512)S(1)}) fusion(f32[512,6400]{1,0:T(8,128)} %get-tuple-element.15, f32[512]{0:T(512)S(1)} %get-tuple-element.14, s32[512]{0:T(512)S(1)} %broadcast_subtract_fusion), kind=kLoop, calls=%fused_computation | loop fusion | flops 22936064 | bytes 13117440 | tf_op jit(solution)/shard_map/reduce_sum | solution.py:37
  111.5 17.6 %all-reduce.1 = (f32[512]{0:T(512)S(1)}, f32[512]{0:T(512)S(1)}, f32[512]{0:T(512)S(1)}) all-reduce(f32[512]{0:T(512)S(1)} %get-tuple-element.13, f32[512]{0:T(512)S(1)} %get-tuple-element.12, f32[512]{0:T(512)S(1)} %get-tuple-element.4), channel_id=1, replica_groups=mesh['tok'=4,'voc'=8] {'voc'}, use_global_device_ids=true, to_apply=%region_9.10 | all-reduce | flops 1536 | bytes 12288 | tf_op jit(solution)/shard_map/psum | solution.py:41
  129.0 0.1 subtract_select_fusion.1
  129.1 0.1 reshape.79
  129.2 65.1 %all-gather.1 = f32[32,2,32]{2,1,0:T(2,128)S(1)} all-gather(f32[1,2,32]{2,1,0:T(2,128)S(1)} %reshape.79), channel_id=1, replica_groups=mesh['tok'=4,'voc'=8] {'tok','voc'}, dimensions={0}, use_global_device_ids=true | all-gather | bytes 8448 | tf_op jit(solution)/shard_map/all_gather | solution.py:54
  194.3 0.1 copy.10
  194.4 0.1 reshape.77
  194.5 63.9 %all-gather = f32[32,2,32]{2,1,0:T(2,128)S(1)} all-gather(f32[1,2,32]{2,1,0:T(2,128)S(1)} %reshape.77), channel_id=1, replica_groups=mesh['tok'=4,'voc'=8] {'tok','voc'}, dimensions={0}, use_global_device_ids=true | all-gather | bytes 8448 | tf_op jit(solution)/shard_map/all_gather | solution.py:53
  258.4 0.1 copy.9
  258.5 0.7 select_reduce_fusion.1
  (5 shorter events, 0.0 us)
Async XLA Ops:
  7.2 55.3 %all-gather.4.cloned.1.call-start = ((), (), s32[]{:S(2)}) async-start(), calls=%async_computation | async-start | bytes 2359296 | tf_op jit(solution)/shard_map/all_gather | solution.py:26
Sparse Core Ops, SparseCore 0:
  10.2 52.1 all-gather.3
where the time goes:
time: 266 us
  blocking collectives  179 us (67%)
  waiting for transfers between devices  34 us (13%)
  matrix products  22.5 us (8%)
  between operations  14.7 us (6%)
  other arithmetic  13.4 us (5%)
    all_gather x1, blocking collectives, shards(): lax.all_gather(entropy_rows, ('tok', 'voc'), axis=0, tiled=True)  65.1 us
    all_gather x1, blocking collectives, shards(): lax.all_gather(logprob_rows, ('tok', 'voc'), axis=0, tiled=True)  63.9 us
    all_gather x1, waiting for transfers between devices, shards(): lax.all_gather(normed, 'voc', axis=0, tiled=True)  34 us
    dot_general x1, matrix products, shards(): jnp.dot(group_matrix, head_weight, preferred_element_type=jnp.float32)  22.5 us
    pmax x1, blocking collectives, shards(): peak_all = lax.pmax(row_peak, 'voc')  18.9 us
    psum x1, blocking collectives, shards(): lax.psum((exp_sum * rescale, exp_dot * rescale, picked), 'voc')  17.6 us
    unnamed x1, blocking collectives  13.2 us
    reduce_sum x1, other arithmetic, shards(): exp_dot = jnp.sum(scaled * logits, axis=1)  7.58 us
  transfers between devices with their start and end apart: 1, of which 1 were waited for; matrix products, arithmetic and copies ran while one was open for 2% of the time, Pallas kernels for 0%

commit v1 on v0

v1 whole, which is shorter than its diff:
```python
import functools

import jax
import jax.numpy as jnp
from jax import lax
from jax.experimental import pallas as pl
from jax.experimental.pallas import tpu as pltpu
from jax.sharding import PartitionSpec as P

EPS = 1e-06
LIVE = 24
RING = 4
LANES = 128
DIGIT = 7
NOWHERE = (1 << (2 * DIGIT)) - 1
TILE = 1280
F32 = jnp.float32
BF16 = jnp.bfloat16
VMEM = pltpu.VMEM
MIB = 2**20


def iota(shape, dim):
    return lax.broadcasted_iota(jnp.int32, shape, dim)


def pack_kernel(n_voc, offset_ref, length_ref, request_ref, hidden_ref, gain_ref, target_ref, out_ref):
    req_dev, span, width = hidden_ref.shape
    rows = req_dev * LIVE
    device = lax.axis_index("tok") * n_voc + lax.axis_index("voc")
    values = hidden_ref[...].reshape(req_dev * span, width).astype(F32)
    square = jnp.mean(values * values, axis=-1, keepdims=True)
    normed = (values * lax.rsqrt(square + EPS) * gain_ref[...]).astype(BF16)
    row = iota((rows, 1), 0)
    source = jnp.zeros((rows, 1), jnp.int32)
    place = jnp.zeros((rows, 1), jnp.int32)
    target = jnp.zeros((rows, 1), F32)
    for slot in range(req_dev):
        step = row - slot * LIVE
        mine = (step >= 0) & (step < LIVE)
        position = offset_ref[slot] + step
        source = jnp.where(mine, slot * span + position, source)
        request = request_ref[device * req_dev + slot]
        scored = jnp.where(step < length_ref[slot], request * span + position, NOWHERE)
        place = jnp.where(mine, scored, place)
        found = mine & (iota((rows, span), 1) == position)
        ids = target_ref[slot : slot + 1, :].astype(F32)
        target += jnp.sum(jnp.where(found, ids, 0.0), axis=1, keepdims=True)
    taken = (iota((rows, req_dev * span), 1) == source).astype(BF16)
    out_ref[:, :width] = jnp.dot(taken, normed, preferred_element_type=F32).astype(BF16)
    target = target.astype(jnp.int32)
    low = (1 << DIGIT) - 1
    digits = (target >> (2 * DIGIT), (target >> DIGIT) & low, target & low, place >> DIGIT, place & low)
    lane = iota((rows, LANES), 1)
    tail = jnp.zeros((rows, LANES), jnp.int32)
    for at, digit in enumerate(digits):
        tail = jnp.where(lane == at, digit, tail)
    out_ref[:, width:] = tail.astype(F32).astype(BF16)


def pack(hidden, norm_gain, lengths, offsets, slot_request, targets, n_voc):
    req_dev, _, width = hidden.shape
    smem = pl.BlockSpec(memory_space=pltpu.SMEM)
    vmem = pl.BlockSpec(memory_space=VMEM)
    return pl.pallas_call(
        functools.partial(pack_kernel, n_voc),
        out_shape=jax.ShapeDtypeStruct((req_dev * LIVE, width + LANES), BF16),
        in_specs=[smem, smem, smem, vmem, vmem, vmem],
        out_specs=vmem,
        compiler_params=pltpu.CompilerParams(vmem_limit_bytes=8 * MIB),
        name="pack",
    )(offsets, lengths, slot_request, hidden, norm_gain.reshape(1, -1), targets)


def decode(tail):
    at, column = iota((LANES, 2 * LANES), 0), iota((LANES, 2 * LANES), 1)
    first = column < LANES
    scale = jnp.zeros((LANES, 2 * LANES), F32)
    for row, value in enumerate((1 << (2 * DIGIT), 1 << DIGIT, 1)):
        scale = jnp.where(first & (at == row), float(value), scale)
    for row, value in enumerate((1 << DIGIT, 1)):
        scale = jnp.where((~first) & (at == row + 3), float(value), scale)
    both = jnp.dot(tail, scale.astype(BF16), preferred_element_type=F32)
    return both[:, :LANES], both[:, LANES:]


def score_kernel(count, carried, per_dev, *refs):
    blocks, weight_ref = refs[:count], refs[count]
    before = refs[count + 1] if carried else None
    out_ref, x_ref, peak_ref, sum_ref, dot_ref, pick_ref, place_ref = refs[count + 1 + carried :]
    size = blocks[0].shape[0]
    rows, width = x_ref.shape
    vocab_dev = weight_ref.shape[1]
    lane = iota((rows, LANES), 1).astype(F32)
    for at, block in enumerate(blocks):
        x_ref[at * size : (at + 1) * size, :] = block[:, :width]
    tails = jnp.concatenate([block[:, width:] for block in blocks], axis=0)
    target, place = decode(tails)
    place_ref[...] = place
    first_column = (lax.axis_index("voc") * vocab_dev).astype(F32)
    wanted = target - lane - first_column
    peak_ref[...] = jnp.full((rows, LANES), -jnp.inf, F32)
    for ref in (sum_ref, dot_ref, pick_ref):
        ref[...] = jnp.zeros((rows, LANES), F32)

    def step(i, _):
        base = pl.multiple_of(i * TILE, TILE)
        logits = jnp.dot(x_ref[...], weight_ref[:, pl.ds(base, TILE)], preferred_element_type=F32)
        parts = [logits[:, at : at + LANES] for at in range(0, TILE, LANES)]
        old = peak_ref[...]
        peak = functools.reduce(jnp.maximum, parts, old)
        drop = jnp.where(i > 0, old - peak, 0.0)
        scale = jnp.exp(drop)
        total = sum_ref[...]
        dots = (dot_ref[...] + drop * total) * scale
        total = total * scale
        pick = pick_ref[...]
        for at, part in enumerate(parts):
            below = part - peak
            weight = jnp.exp(below)
            total += weight
            dots += weight * below
            pick = jnp.where(wanted == (base + at * LANES).astype(F32), part, pick)
        peak_ref[...] = peak
        sum_ref[...] = total
        dot_ref[...] = dots
        pick_ref[...] = pick
        return 0

    lax.fori_loop(0, vocab_dev // TILE, step, 0)
    peak = jnp.max(peak_ref[...], axis=1, keepdims=True)
    drop = peak_ref[...] - peak
    scale = jnp.exp(drop)
    total = jnp.sum(sum_ref[...] * scale, axis=1, keepdims=True)
    dots = jnp.sum((dot_ref[...] + drop * sum_ref[...]) * scale, axis=1, keepdims=True)
    pick = jnp.sum(pick_ref[...], axis=1, keepdims=True)
    stats = jnp.zeros((rows, LANES), F32)
    for at, value in enumerate((peak, total, dots, pick)):
        high = value.astype(BF16).astype(F32)
        middle = (value - high).astype(BF16).astype(F32)
        low = value - high - middle
        for part, piece in enumerate((high, middle, low)):
            stats = jnp.where(lane == float(8 * part + at), piece, stats)
    stats = stats.T.astype(BF16)[:32]
    for group in range(out_ref.shape[0] * per_dev // LANES):
        there = (place_ref[...] == lane + float(group * LANES)).astype(F32).astype(BF16)
        moved = jnp.dot(stats, there, preferred_element_type=F32)
        moved = moved[0:8] + moved[8:16] + moved[16:24]
        for at in range(LANES // per_dev):
            to = group * (LANES // per_dev) + at
            part = moved[:, at * per_dev : (at + 1) * per_dev]
            if carried:
                part += before[to, :, :per_dev]
            out_ref[to, :, :per_dev] = part


def score(blocks, weight, before, n_dev, per_dev):
    count = len(blocks)
    size, wide = blocks[0].shape
    rows, width = count * size, wide - LANES
    operands = [pltpu.with_memory_space_constraint(a, VMEM) for a in (*blocks, weight)]
    if before is not None:
        operands.append(before)
    vmem = pl.BlockSpec(memory_space=VMEM)
    state = VMEM((rows, LANES), F32)
    vocab_dev = weight.shape[1]
    return pl.pallas_call(
        functools.partial(score_kernel, count, before is not None, per_dev),
        out_shape=jax.ShapeDtypeStruct((n_dev, 8, LANES), F32),
        in_specs=[vmem] * len(operands),
        out_specs=vmem,
        scratch_shapes=[VMEM((rows, width), BF16)] + [state] * 5,
        compiler_params=pltpu.CompilerParams(vmem_limit_bytes=16 * MIB),
        cost_estimate=pl.CostEstimate(
            flops=2 * rows * width * vocab_dev,
            bytes_accessed=2 * width * vocab_dev,
            transcendentals=rows * vocab_dev,
        ),
        name="score",
    )(*operands)


def finish_kernel(all_ref, logprob_ref, entropy_ref):
    req_dev, span = logprob_ref.shape
    peak, total, dots, pick = (all_ref[:, at, :] for at in range(4))
    held = total > 0.0
    top = jnp.max(jnp.where(held, peak, -jnp.inf), axis=0, keepdims=True)
    scored = top > -jnp.inf
    top = jnp.where(scored, top, 0.0)
    drop = jnp.where(held, peak - top, 0.0)
    scale = jnp.exp(drop)
    whole = jnp.sum(total * scale, axis=0, keepdims=True)
    whole = jnp.where(scored, whole, 1.0)
    mean = jnp.sum((dots + drop * total) * scale, axis=0, keepdims=True) / whole
    log_total = jnp.log(whole)
    logprob = jnp.where(scored, jnp.sum(pick, axis=0, keepdims=True) - top - log_total, 0.0)
    entropy = jnp.where(scored, log_total - mean, 0.0)
    for at in range(req_dev):
        logprob_ref[at : at + 1, :] = logprob[:, at * span : (at + 1) * span]
        entropy_ref[at : at + 1, :] = entropy[:, at * span : (at + 1) * span]


def finish(everything, req_dev, span):
    vmem = pl.BlockSpec(memory_space=VMEM)
    shape = jax.ShapeDtypeStruct((req_dev, span), F32)
    return pl.pallas_call(
        finish_kernel,
        out_shape=(shape, shape),
        in_specs=[vmem],
        out_specs=(vmem, vmem),
        compiler_params=pltpu.CompilerParams(vmem_limit_bytes=8 * MIB),
        name="finish",
    )(everything)


def shift(block, along_z, along_y, n_voc):
    side = n_voc // RING
    pairs = [
        (z * side + y, (z + along_z) % RING * side + (y + along_y) % side)
        for z in range(RING)
        for y in range(side)
    ]
    return lax.ppermute(block, "voc", pairs)


def shards(n_tok, n_voc, hidden, norm_gain, head_weight, lengths, offsets, slot_request, targets):
    req_dev, span, _ = hidden.shape
    n_dev = n_tok * n_voc
    own = pack(hidden, norm_gain, lengths, offsets, slot_request, targets, n_voc)
    side = n_voc // RING
    steps = [(z, y) for z in range(RING) for y in range(side)]
    steps.sort(key=lambda at: (min(at[0], RING - at[0]) + min(at[1], side - at[1]), at[0]))
    blocks = [own] + [shift(own, z, y, n_voc) for z, y in steps[1:]]
    half = len(blocks) // 2
    sent = score(blocks[:half], head_weight, None, n_dev, req_dev * span)
    sent = score(blocks[half:], head_weight, sent, n_dev, req_dev * span)
    everything = lax.all_to_all(sent, ("tok", "voc"), 0, 0, tiled=True)
    return finish(everything, req_dev, span)


def solution(mesh):
    placed = (
        P(("tok", "voc"), None, None),
        P(),
        P(None, "voc"),
        P(("tok", "voc")),
        P(("tok", "voc")),
        P(),
        P(("tok", "voc"), None),
    )
    return jax.shard_map(
        functools.partial(shards, mesh.shape["tok"], mesh.shape["voc"]),
        mesh=mesh,
        in_specs=placed,
        out_specs=(P(("tok", "voc"), None), P(("tok", "voc"), None)),
        check_vma=False,
    )
```

time: 266 us -> 75.8 us (0.28)
  blocking collectives: 179 us -> 11.5 us
  waiting for transfers between devices: 34 us -> 8.7 us
  matrix products: 22.5 us -> 0 us
  local copies, waits for them, and re-layouts: 2.62 us -> 21.2 us
  Pallas kernels: 0 us -> 17.9 us
  starting transfers between devices: 0.04 us -> 15.5 us
  between operations: 14.7 us -> 0.66 us
  other arithmetic: 13.4 us -> 0 us
    all_gather x2 -> x0, blocking collectives: 129 us -> none  [the longest x1 65.1 us: shards(): lax.all_gather(entropy_rows, ('tok', 'voc'), axis=0, tiled=True)]
    all_gather x1 -> x0, waiting for transfers between devices: 34 us -> none  [shards(): lax.all_gather(normed, 'voc', axis=0, tiled=True)]
    dot_general x1 -> x0, matrix products: 22.5 us -> none  [shards(): jnp.dot(group_matrix, head_weight, preferred_element_type=jnp.float32)]
    unnamed x7 -> x16, local copies, waits for them, and re-layouts: 1.78 us -> 21.2 us
    pmax x1 -> x0, blocking collectives: 18.9 us -> none  [shards(): peak_all = lax.pmax(row_peak, 'voc')]
    pallas_call x0 -> x4, Pallas kernels: none -> 17.9 us  [the longest x2 16.3 us: score(): pl.pallas_call(functools.partial(score_kernel, count, before is not None,...]
    psum x1 -> x0, blocking collectives: 17.6 us -> none  [shards(): lax.psum((exp_sum * rescale, exp_dot * rescale, picked), 'voc')]
    ppermute x0 -> x7, starting transfers between devices: none -> 15.5 us  [shift(): return lax.ppermute(block, 'voc', pairs)]
  transfers between devices with their start and end apart: 1 -> 7, of which waited for: 1 -> 3; matrix products, arithmetic and copies ran while one was open for 2% -> 0% of each run, Pallas kernels for 0% -> 11%
where the time goes in v1:
time: 75.8 us; the launch traced here: 75.5 us
  local copies, waits for them, and re-layouts  21.2 us (28%)
  Pallas kernels  17.9 us (24%)
  starting transfers between devices  15.5 us (20%)
  blocking collectives  11.5 us (15%)
  waiting for transfers between devices  8.7 us (11%)
    unnamed x16, local copies, waits for them, and re-layouts  21.2 us
    pallas_call x2, Pallas kernels, score(): pl.pallas_call(functools.partial(score_kernel, count, before is not None,...  16.3 us
    ppermute x7, starting transfers between devices, shift(): return lax.ppermute(block, 'voc', pairs)  15.5 us
    all_to_all x1, blocking collectives, shards(): everything = lax.all_to_all(sent, ('tok', 'voc'), 0, 0, tiled=True)  11.5 us
    ppermute x7, waiting for transfers between devices, shift(): return lax.ppermute(block, 'voc', pairs)  8.7 us
  transfers between devices with their start and end apart: 7, of which 3 were waited for; matrix products, arithmetic and copies ran while one was open for 0% of the time, Pallas kernels for 11%

profile of v1, /device:TPU:0, one launch (start us, length us, event | category | flops | bytes accessed | tf_op | source)
XLA Modules:
  0.0 75.5 jit_solution(8276408637946544318)
XLA Ops:
  0.6 0.0 copy-start.2
  0.6 0.9 %copy-done.2 = bf16[2,32,2048]{2,1,0:T(8,128)(2,1)S(1)} copy-done((bf16[2,32,2048]{2,1,0:T(8,128)(2,1)S(1)}, bf16[2,32,2048]{2,1,0:T(8,128)(2,1)}, u32[]{:S(2)}) %copy-start.2) | copy-done | bytes 262168
  1.6 0.0 copy-start.3
  1.6 0.7 copy-done.3
  2.3 0.0 copy-start.4
  2.3 0.7 copy-done.4
  3.0 0.0 copy-start.5
  3.0 0.7 copy-done.5
  3.6 0.0 copy-start.6
  3.6 0.7 copy-done.6
  4.3 0.0 copy-start.7
  4.3 0.7 copy-done.7
  4.9 0.9 %pack.1.refs_0_ = bf16[48,2176]{1,0:T(8,128)(2,1)S(1)} custom-call(s32[2]{0:T(128)S(1)} %copy-done.5, s32[2]{0:T(128)S(1)} %copy-done.6, s32[64]{0:T(128)S(1)} %copy-done.7, bf16[2,32,2048]{2,1,0:T(8,128)(2,1)S(1)} %copy-done.2, f32[1,2048]{1,0:T(1,128)S(1)} %bitcast.1, s32[2,32]{1,0:T(2,128)S(1)} %copy-done.4), custom_call_target="tpu_custom_call" | custom-call | tf_op jit(solution)/shard_map/pack/pallas_call | solution.py:65
  5.8 5.1 %collective-permute-start.6 = (bf16[48,2176]{1,0:T(8,128)(2,1)S(1)}, bf16[48,2176]{1,0:T(8,128)(2,1)S(1)}, u32[]{:S(2)}, u32[]{:S(2)}) collective-permute-start(bf16[48,2176]{1,0:T(8,128)(2,1)S(1)} %pack.1.refs_0_), channel_id=1, source_target_pairs={{0,6},{1,7},{2,0},{3,1},{4,2},{5,3},{6,4},{7,5},{8,14},{9,15},{10,... | collective-permute-start | bytes 626696 | tf_op jit(solution)/shard_map/ppermute | solution.py:223
  10.9 0.0 collective-permute-start.5
  10.9 1.5 %collective-permute-start.4 = (bf16[48,2176]{1,0:T(8,128)(2,1)S(1)}, bf16[48,2176]{1,0:T(8,128)(2,1)S(1)}, u32[]{:S(2)}, u32[]{:S(2)}) collective-permute-start(bf16[48,2176]{1,0:T(8,128)(2,1)S(1)} %pack.1.refs_0_), channel_id=1, source_target_pairs={{0,1},{1,0},{2,3},{3,2},{4,5},{5,4},{6,7},{7,6},{8,9},{9,8},{10,11... | collective-permute-start | bytes 626696 | tf_op jit(solution)/shard_map/ppermute | solution.py:223
  12.4 1.0 %collective-permute-start.3 = (bf16[48,2176]{1,0:T(8,128)(2,1)S(1)}, bf16[48,2176]{1,0:T(8,128)(2,1)S(1)}, u32[]{:S(2)}, u32[]{:S(2)}) collective-permute-start(bf16[48,2176]{1,0:T(8,128)(2,1)S(1)} %pack.1.refs_0_), channel_id=1, source_target_pairs={{0,5},{1,4},{2,7},{3,6},{4,1},{5,0},{6,3},{7,2},{8,13},{9,12},{10,... | collective-permute-start | bytes 626696 | tf_op jit(solution)/shard_map/ppermute | solution.py:223
  13.4 2.8 %collective-permute-start.2 = (bf16[48,2176]{1,0:T(8,128)(2,1)S(1)}, bf16[48,2176]{1,0:T(8,128)(2,1)S(1)}, u32[]{:S(2)}, u32[]{:S(2)}) collective-permute-start(bf16[48,2176]{1,0:T(8,128)(2,1)S(1)} %pack.1.refs_0_), channel_id=1, source_target_pairs={{0,7},{1,6},{2,1},{3,0},{4,3},{5,2},{6,5},{7,4},{8,15},{9,14},{10,... | collective-permute-start | bytes 626696 | tf_op jit(solution)/shard_map/ppermute | solution.py:223
  16.2 0.3 collective-permute-done.6.refs_3_
  16.5 2.7 %collective-permute-start.1 = (bf16[48,2176]{1,0:T(8,128)(2,1)S(1)}, bf16[48,2176]{1,0:T(8,128)(2,1)S(1)}, u32[]{:S(2)}, u32[]{:S(2)}) collective-permute-start(bf16[48,2176]{1,0:T(8,128)(2,1)S(1)} %pack.1.refs_0_), channel_id=1, source_target_pairs={{0,4},{1,5},{2,6},{3,7},{4,0},{5,1},{6,2},{7,3},{8,12},{9,13},{10,... | collective-permute-start | bytes 626696 | tf_op jit(solution)/shard_map/ppermute | solution.py:223
  19.2 2.8 %collective-permute-done.5.refs_2_ = bf16[48,2176]{1,0:T(8,128)(2,1)S(1)} collective-permute-done((bf16[48,2176]{1,0:T(8,128)(2,1)S(1)}, bf16[48,2176]{1,0:T(8,128)(2,1)S(1)}, u32[]{:S(2)}, u32[]{:S(2)}) %collective-permute-start.5) | collective-permute-done | bytes 208928 | tf_op jit(solution)/shard_map/ppermute | solution.py:223
  22.0 2.4 %collective-permute-start = (bf16[48,2176]{1,0:T(8,128)(2,1)S(1)}, bf16[48,2176]{1,0:T(8,128)(2,1)S(1)}, u32[]{:S(2)}, u32[]{:S(2)}) collective-permute-start(bf16[48,2176]{1,0:T(8,128)(2,1)S(1)} %pack.1.refs_0_), channel_id=1, source_target_pairs={{0,3},{1,2},{2,5},{3,4},{4,7},{5,6},{6,1},{7,0},{8,11},{9,10},{10,... | collective-permute-start | bytes 626696 | tf_op jit(solution)/shard_map/ppermute | solution.py:223
  24.4 0.0 collective-permute-done.4.refs_1_
  24.4 0.0 copy-start
  24.4 8.5 %copy-done = bf16[2048,6400]{1,0:T(8,128)(2,1)S(1)} copy-done((bf16[2048,6400]{1,0:T(8,128)(2,1)S(1)}, bf16[2048,6400]{1,0:T(8,128)(2,1)}, u32[]{:S(2)}) %copy-start) | copy-done | bytes 26214424
  32.9 8.2 %score.2.refs_5_ = f32[32,8,128]{2,1,0:T(8,128)S(1)} custom-call(bf16[48,2176]{1,0:T(8,128)(2,1)S(1)} %pack.1.refs_0_, bf16[48,2176]{1,0:T(8,128)(2,1)S(1)} %collective-permute-done.4.refs_1_, bf16[48,2176]{1,0:T(8,128)(2,1)S(1)} %collective-permute-done.5.refs_2_, bf16[48,2176]{1,0:T(8,128)(2,1)S(1)} %collective-permute-done.6.refs_3_, ...), custom_call_target="tpu_custom_call" | custom-call | flops 5033164800 | bytes 26214400 | tf_op jit(solution)/shard_map/score/pallas_call | solution.py:167
  41.0 0.0 collective-permute-done.3.refs_3_
  41.0 0.0 collective-permute-done.2.refs_2_
  41.0 5.6 %collective-permute-done.1.refs_1_ = bf16[48,2176]{1,0:T(8,128)(2,1)S(1)} collective-permute-done((bf16[48,2176]{1,0:T(8,128)(2,1)S(1)}, bf16[48,2176]{1,0:T(8,128)(2,1)S(1)}, u32[]{:S(2)}, u32[]{:S(2)}) %collective-permute-start.1) | collective-permute-done | bytes 208928 | tf_op jit(solution)/shard_map/ppermute | solution.py:223
  46.6 0.0 collective-permute-done.refs_0_
  46.6 0.0 copy-start.1
  46.6 8.5 %copy-done.1 = bf16[2048,6400]{1,0:T(8,128)(2,1)S(1)} copy-done((bf16[2048,6400]{1,0:T(8,128)(2,1)S(1)}, bf16[2048,6400]{1,0:T(8,128)(2,1)}, u32[]{:S(2)}) %copy-start.1) | copy-done | bytes 26214424
  55.1 8.2 %score.3 = f32[32,8,128]{2,1,0:T(8,128)S(1)} custom-call(bf16[48,2176]{1,0:T(8,128)(2,1)S(1)} %collective-permute-done.refs_0_, bf16[48,2176]{1,0:T(8,128)(2,1)S(1)} %collective-permute-done.1.refs_1_, bf16[48,2176]{1,0:T(8,128)(2,1)S(1)} %collective-permute-done.2.refs_2_, bf16[48,2176]{1,0:T(8,128)(2,1)S(1)} %collective-permute-done.3.refs_3_, ...), custom_call_target="tpu_custom_call" | custom-call | flops 5033164800 | bytes 26214400 | tf_op jit(solution)/shard_map/score/pallas_call | solution.py:167
  63.2 11.5 %all_to_all.5.all_ref = f32[32,8,128]{2,1,0:T(8,128)S(1)} all-to-all(f32[32,8,128]{2,1,0:T(8,128)S(1)} %score.3), channel_id=1, replica_groups=mesh['tok'=4,'voc'=8] {'tok','voc'}, dimensions={0} | all-to-all | bytes 262144 | tf_op jit(solution)/shard_map/all_to_all | solution.py:237
  74.8 0.7 finish.1
Async XLA Ops:
  0.6 1.0 %copy-start.2 = (bf16[2,32,2048]{2,1,0:T(8,128)(2,1)S(1)}, bf16[2,32,2048]{2,1,0:T(8,128)(2,1)}, u32[]{:S(2)}) copy-start(bf16[2,32,2048]{2,1,0:T(8,128)(2,1)} %hidden_ref.1) | copy-start | bytes 786436
  1.6 0.7 copy-start.3
  2.3 0.7 copy-start.4
  3.0 0.7 copy-start.5
  3.6 0.7 copy-start.6
  4.3 0.7 copy-start.7
  5.8 10.7 %collective-permute-start.6 = (bf16[48,2176]{1,0:T(8,128)(2,1)S(1)}, bf16[48,2176]{1,0:T(8,128)(2,1)S(1)}, u32[]{:S(2)}, u32[]{:S(2)}) collective-permute-start(bf16[48,2176]{1,0:T(8,128)(2,1)S(1)} %pack.1.refs_0_), channel_id=1, source_target_pairs={{0,6},{1,7},{2,0},{3,1},{4,2},{5,3},{6,4},{7,5},{8,14},{9,15},{10,... | collective-permute-start | bytes 626696 | tf_op jit(solution)/shard_map/ppermute | solution.py:223
  10.9 11.1 %collective-permute-start.5 = (bf16[48,2176]{1,0:T(8,128)(2,1)S(1)}, bf16[48,2176]{1,0:T(8,128)(2,1)S(1)}, u32[]{:S(2)}, u32[]{:S(2)}) collective-permute-start(bf16[48,2176]{1,0:T(8,128)(2,1)S(1)} %pack.1.refs_0_), channel_id=1, source_target_pairs={{0,2},{1,3},{2,4},{3,5},{4,6},{5,7},{6,0},{7,1},{8,10},{9,11},{10,... | collective-permute-start | bytes 626696 | tf_op jit(solution)/shard_map/ppermute | solution.py:223
  10.9 13.5 %collective-permute-start.4 = (bf16[48,2176]{1,0:T(8,128)(2,1)S(1)}, bf16[48,2176]{1,0:T(8,128)(2,1)S(1)}, u32[]{:S(2)}, u32[]{:S(2)}) collective-permute-start(bf16[48,2176]{1,0:T(8,128)(2,1)S(1)} %pack.1.refs_0_), channel_id=1, source_target_pairs={{0,1},{1,0},{2,3},{3,2},{4,5},{5,4},{6,7},{7,6},{8,9},{9,8},{10,11... | collective-permute-start | bytes 626696 | tf_op jit(solution)/shard_map/ppermute | solution.py:223
  12.4 28.6 %collective-permute-start.3 = (bf16[48,2176]{1,0:T(8,128)(2,1)S(1)}, bf16[48,2176]{1,0:T(8,128)(2,1)S(1)}, u32[]{:S(2)}, u32[]{:S(2)}) collective-permute-start(bf16[48,2176]{1,0:T(8,128)(2,1)S(1)} %pack.1.refs_0_), channel_id=1, source_target_pairs={{0,5},{1,4},{2,7},{3,6},{4,1},{5,0},{6,3},{7,2},{8,13},{9,12},{10,... | collective-permute-start | bytes 626696 | tf_op jit(solution)/shard_map/ppermute | solution.py:223
  13.4 27.6 %collective-permute-start.2 = (bf16[48,2176]{1,0:T(8,128)(2,1)S(1)}, bf16[48,2176]{1,0:T(8,128)(2,1)S(1)}, u32[]{:S(2)}, u32[]{:S(2)}) collective-permute-start(bf16[48,2176]{1,0:T(8,128)(2,1)S(1)} %pack.1.refs_0_), channel_id=1, source_target_pairs={{0,7},{1,6},{2,1},{3,0},{4,3},{5,2},{6,5},{7,4},{8,15},{9,14},{10,... | collective-permute-start | bytes 626696 | tf_op jit(solution)/shard_map/ppermute | solution.py:223
  16.5 30.1 %collective-permute-start.1 = (bf16[48,2176]{1,0:T(8,128)(2,1)S(1)}, bf16[48,2176]{1,0:T(8,128)(2,1)S(1)}, u32[]{:S(2)}, u32[]{:S(2)}) collective-permute-start(bf16[48,2176]{1,0:T(8,128)(2,1)S(1)} %pack.1.refs_0_), channel_id=1, source_target_pairs={{0,4},{1,5},{2,6},{3,7},{4,0},{5,1},{6,2},{7,3},{8,12},{9,13},{10,... | collective-permute-start | bytes 626696 | tf_op jit(solution)/shard_map/ppermute | solution.py:223
  22.0 24.6 %collective-permute-start = (bf16[48,2176]{1,0:T(8,128)(2,1)S(1)}, bf16[48,2176]{1,0:T(8,128)(2,1)S(1)}, u32[]{:S(2)}, u32[]{:S(2)}) collective-permute-start(bf16[48,2176]{1,0:T(8,128)(2,1)S(1)} %pack.1.refs_0_), channel_id=1, source_target_pairs={{0,3},{1,2},{2,5},{3,4},{4,7},{5,6},{6,1},{7,0},{8,11},{9,10},{10,... | collective-permute-start | bytes 626696 | tf_op jit(solution)/shard_map/ppermute | solution.py:223
  24.4 8.5 %copy-start = (bf16[2048,6400]{1,0:T(8,128)(2,1)S(1)}, bf16[2048,6400]{1,0:T(8,128)(2,1)}, u32[]{:S(2)}) copy-start(bf16[2048,6400]{1,0:T(8,128)(2,1)} %refs_4_.3) | copy-start | bytes 78643200
  46.6 8.5 %copy-start.1 = (bf16[2048,6400]{1,0:T(8,128)(2,1)S(1)}, bf16[2048,6400]{1,0:T(8,128)(2,1)}, u32[]{:S(2)}) copy-start(bf16[2048,6400]{1,0:T(8,128)(2,1)} %refs_4_.3) | copy-start | bytes 78643200

commit v2 on v1

--- a/solution.py
+++ b/solution.py
@@ -13,7 +13,11 @@
 LANES = 128
 DIGIT = 7
 NOWHERE = (1 << (2 * DIGIT)) - 1
+STATS = 4
 TILE = 1280
+PIECE = 512
+AHEAD = 4
+MOST = 4
 F32 = jnp.float32
 BF16 = jnp.bfloat16
 VMEM = pltpu.VMEM
@@ -24,7 +28,14 @@
     return lax.broadcasted_iota(jnp.int32, shape, dim)
 
 
-def pack_kernel(n_voc, offset_ref, length_ref, request_ref, hidden_ref, gain_ref, target_ref, out_ref):
+def pack_kernel(n_voc, *refs):
+    sources, out_ref, copies, sems = refs[:6], refs[6], refs[7:13], refs[13]
+    started = [pltpu.make_async_copy(a, b, sems.at[at]) for at, (a, b) in enumerate(zip(sources, copies))]
+    for copy in started:
+        copy.start()
+    for copy in started:
+        copy.wait()
+    offset_ref, length_ref, request_ref, hidden_ref, gain_ref, target_ref = copies
     req_dev, span, width = hidden_ref.shape
     rows = req_dev * LIVE
     device = lax.axis_index("tok") * n_voc + lax.axis_index("voc")
@@ -60,16 +71,18 @@
 
 def pack(hidden, norm_gain, lengths, offsets, slot_request, targets, n_voc):
     req_dev, _, width = hidden.shape
-    smem = pl.BlockSpec(memory_space=pltpu.SMEM)
-    vmem = pl.BlockSpec(memory_space=VMEM)
+    arrays = (offsets, lengths, slot_request, hidden, norm_gain.reshape(1, -1), targets)
+    spaces = (pltpu.SMEM,) * 3 + (VMEM,) * 3
     return pl.pallas_call(
         functools.partial(pack_kernel, n_voc),
         out_shape=jax.ShapeDtypeStruct((req_dev * LIVE, width + LANES), BF16),
-        in_specs=[smem, smem, smem, vmem, vmem, vmem],
-        out_specs=vmem,
+        in_specs=[pl.BlockSpec(memory_space=pl.ANY)] * 6,
+        out_specs=pl.BlockSpec(memory_space=VMEM),
+        scratch_shapes=[space(a.shape, a.dtype) for space, a in zip(spaces, arrays)]
+        + [pltpu.SemaphoreType.DMA((6,))],
         compiler_params=pltpu.CompilerParams(vmem_limit_bytes=8 * MIB),
         name="pack",
-    )(offsets, lengths, slot_request, hidden, norm_gain.reshape(1, -1), targets)
+    )(*(pltpu.with_memory_space_constraint(a, pltpu.HBM) for a in arrays))
 
 
 def decode(tail):
@@ -84,50 +97,50 @@
     return both[:, :LANES], both[:, LANES:]
 
 
-def score_kernel(count, carried, per_dev, *refs):
-    blocks, weight_ref = refs[:count], refs[count]
-    before = refs[count + 1] if carried else None
-    out_ref, x_ref, peak_ref, sum_ref, dot_ref, pick_ref, place_ref = refs[count + 1 + carried :]
-    size = blocks[0].shape[0]
-    rows, width = x_ref.shape
-    vocab_dev = weight_ref.shape[1]
-    lane = iota((rows, LANES), 1).astype(F32)
+def tiles(columns, size):
+    return [(base, min(size, columns - base)) for base in range(0, columns, size)]
+
+
+def assemble(blocks, x_ref, place_ref):
+    size, width = blocks[0].shape[0], x_ref.shape[1]
     for at, block in enumerate(blocks):
         x_ref[at * size : (at + 1) * size, :] = block[:, :width]
-    tails = jnp.concatenate([block[:, width:] for block in blocks], axis=0)
-    target, place = decode(tails)
+    target, place = decode(jnp.concatenate([block[:, width:] for block in blocks], axis=0))
     place_ref[...] = place
-    first_column = (lax.axis_index("voc") * vocab_dev).astype(F32)
-    wanted = target - lane - first_column
-    peak_ref[...] = jnp.full((rows, LANES), -jnp.inf, F32)
-    for ref in (sum_ref, dot_ref, pick_ref):
-        ref[...] = jnp.zeros((rows, LANES), F32)
-
-    def step(i, _):
-        base = pl.multiple_of(i * TILE, TILE)
-        logits = jnp.dot(x_ref[...], weight_ref[:, pl.ds(base, TILE)], preferred_element_type=F32)
-        parts = [logits[:, at : at + LANES] for at in range(0, TILE, LANES)]
+    return target
+
+
+def take(logits_ref, state, wanted, base, wide, fresh):
+    peak_ref, sum_ref, dot_ref, pick_ref = state
+    peak = functools.reduce(jnp.maximum, [logits_ref[:, at : at + LANES] for at in range(0, wide, LANES)])
+    if fresh:
+        total = dots = pick = jnp.zeros_like(peak)
+    else:
         old = peak_ref[...]
-        peak = functools.reduce(jnp.maximum, parts, old)
-        drop = jnp.where(i > 0, old - peak, 0.0)
+        peak = jnp.maximum(old, peak)
+        drop = old - peak
         scale = jnp.exp(drop)
         total = sum_ref[...]
         dots = (dot_ref[...] + drop * total) * scale
         total = total * scale
         pick = pick_ref[...]
-        for at, part in enumerate(parts):
-            below = part - peak
-            weight = jnp.exp(below)
-            total += weight
-            dots += weight * below
-            pick = jnp.where(wanted == (base + at * LANES).astype(F32), part, pick)
-        peak_ref[...] = peak
-        sum_ref[...] = total
-        dot_ref[...] = dots
-        pick_ref[...] = pick
-        return 0
-
-    lax.fori_loop(0, vocab_dev // TILE, step, 0)
+    for at in range(0, wide, LANES):
+        part = logits_ref[:, at : at + LANES]
+        below = part - peak
+        weight = jnp.exp(below)
+        total += weight
+        dots += weight * below
+        pick = jnp.where(wanted == float(base + at), part, pick)
+    peak_ref[...] = peak
+    sum_ref[...] = total
+    dot_ref[...] = dots
+    pick_ref[...] = pick
+
+
+def route(state, place_ref, before_ref, out_ref, per_dev):
+    peak_ref, sum_ref, dot_ref, pick_ref = state
+    rows = place_ref.shape[0]
+    lane = iota((rows, LANES), 1).astype(F32)
     peak = jnp.max(peak_ref[...], axis=1, keepdims=True)
     drop = peak_ref[...] - peak
     scale = jnp.exp(drop)
@@ -145,32 +158,129 @@
     for group in range(out_ref.shape[0] * per_dev // LANES):
         there = (place_ref[...] == lane + float(group * LANES)).astype(F32).astype(BF16)
         moved = jnp.dot(stats, there, preferred_element_type=F32)
-        moved = moved[0:8] + moved[8:16] + moved[16:24]
+        moved = (moved[0:8] + moved[8:16] + moved[16:24])[:STATS]
         for at in range(LANES // per_dev):
             to = group * (LANES // per_dev) + at
             part = moved[:, at * per_dev : (at + 1) * per_dev]
-            if carried:
-                part += before[to, :, :per_dev]
+            if before_ref is not None:
+                part += before_ref[to, :, :per_dev]
             out_ref[to, :, :per_dev] = part
 
 
-def score(blocks, weight, before, n_dev, per_dev):
+def sweep(x_ref, plan, logits, state, wanted, fresh):
+    last = None
+    for at, (weight_ref, column, base, wide, wait) in enumerate(plan):
+        wait()
+        logits[at % 2][:, :wide] = jnp.dot(
+            x_ref[...], weight_ref[:, column : column + wide], preferred_element_type=F32
+        )
+        if last is not None:
+            take(logits[(at - 1) % 2], state, wanted, *last, fresh and at == 1)
+        last = (base, wide)
+    take(logits[(len(plan) - 1) % 2], state, wanted, *last, fresh and len(plan) == 1)
+
+
+def wanted_columns(target, vocab_dev):
+    first = (lax.axis_index("voc") * vocab_dev).astype(F32)
+    return target - first - iota(target.shape, 1).astype(F32)
+
+
+def load_kernel(count, lo, hi, per_dev, *refs):
+    last = hi is None
+    blocks, (weight_ref, *refs) = refs[:count], refs[count:]
+    if last:
+        before_ref, out_ref, held_ref, *refs = refs
+    else:
+        state_ref, held_ref, *refs = refs
+    x_ref, place_ref, even_ref, odd_ref, sems, *refs = refs
+    vocab_dev = weight_ref.shape[1]
+    hi = vocab_dev if last else hi
+    plan = tiles(hi - lo, PIECE)
+    fetches = [
+        pltpu.make_async_copy(
+            weight_ref.at[:, pl.ds(lo + base, wide)], held_ref.at[:, pl.ds(base, wide)], sems.at[at]
+        )
+        for at, (base, wide) in enumerate(plan)
+    ]
+    for fetch in fetches[:AHEAD]:
+        fetch.start()
+    target = assemble(blocks, x_ref, place_ref)
+    state = refs if last else [state_ref.at[at] for at in range(STATS)]
+    if last:
+        for at in range(STATS):
+            state[at][...] = before_ref[at]
+
+    def arrival(at):
+        def wait():
+            fetches[at].wait()
+            if at + AHEAD < len(fetches):
+                fetches[at + AHEAD].start()
+
+        return wait
+
+    steps = [(held_ref, base, lo + base, wide, arrival(at)) for at, (base, wide) in enumerate(plan)]
+    sweep(x_ref, steps, (even_ref, odd_ref), state, wanted_columns(target, vocab_dev), not last)
+    if last:
+        route(state, place_ref, None, out_ref, per_dev)
+
+
+def load(blocks, weight, before, lo, hi, n_dev, per_dev):
+    rows, width = len(blocks) * blocks[0].shape[0], blocks[0].shape[1] - LANES
+    vocab_dev = weight.shape[1]
+    last = before is not None
+    count = (vocab_dev if last else hi) - lo
+    vmem = pl.BlockSpec(memory_space=VMEM)
+    result = (n_dev, STATS, LANES) if last else (STATS, rows, LANES)
+    operands = [pltpu.with_memory_space_constraint(a, VMEM) for a in blocks]
+    operands.append(pltpu.with_memory_space_constraint(weight, pltpu.HBM))
+    operands += [before] if last else []
+    state = VMEM((rows, LANES), F32)
+    return pl.pallas_call(
+        functools.partial(load_kernel, len(blocks), lo, None if last else hi, per_dev),
+        out_shape=(jax.ShapeDtypeStruct(result, F32), VMEM((width, count), BF16)),
+        in_specs=[vmem] * len(blocks) + [pl.BlockSpec(memory_space=pl.ANY)] + [vmem] * last,
+        out_specs=(vmem, vmem),
+        scratch_shapes=[VMEM((rows, width), BF16), state]
+        + [VMEM((rows, PIECE), F32)] * 2
+        + [pltpu.SemaphoreType.DMA((len(tiles(count, PIECE)),))]
+        + [state] * (STATS * last),
+        compiler_params=pltpu.CompilerParams(vmem_limit_bytes=6 * MIB),
+        cost_estimate=pl.CostEstimate(
+            flops=2 * rows * width * count, bytes_accessed=2 * width * count, transcendentals=rows * count
+        ),
+        name="load",
+    )(*operands)
+
+
+def score_kernel(count, carried, per_dev, *refs):
+    blocks, (first_ref, second_ref, *refs) = refs[:count], refs[count:]
+    if carried:
+        before_ref, *refs = refs
+    out_ref, x_ref, place_ref, even_ref, odd_ref, *state = refs
+    cut = first_ref.shape[1]
+    target = assemble(blocks, x_ref, place_ref)
+    steps = [(first_ref, base, base, wide, lambda: None) for base, wide in tiles(cut, TILE)]
+    steps += [(second_ref, base, cut + base, wide, lambda: None) for base, wide in tiles(second_ref.shape[1], TILE)]
+    wanted = wanted_columns(target, cut + second_ref.shape[1])
+    sweep(x_ref, steps, (even_ref, odd_ref), state, wanted, True)
+    route(state, place_ref, before_ref if carried else None, out_ref, per_dev)
+
+
+def score(blocks, weights, before, n_dev, per_dev):
     count = len(blocks)
-    size, wide = blocks[0].shape
-    rows, width = count * size, wide - LANES
-    operands = [pltpu.with_memory_space_constraint(a, VMEM) for a in (*blocks, weight)]
-    if before is not None:
-        operands.append(before)
+    rows, width = count * blocks[0].shape[0], blocks[0].shape[1] - LANES
+    vocab_dev = sum(a.shape[1] for a in weights)
     vmem = pl.BlockSpec(memory_space=VMEM)
+    operands = [pltpu.with_memory_space_constraint(a, VMEM) for a in (*blocks, *weights)]
+    operands += [] if before is None else [before]
     state = VMEM((rows, LANES), F32)
-    vocab_dev = weight.shape[1]
     return pl.pallas_call(
         functools.partial(score_kernel, count, before is not None, per_dev),
-        out_shape=jax.ShapeDtypeStruct((n_dev, 8, LANES), F32),
+        out_shape=jax.ShapeDtypeStruct((n_dev, STATS, LANES), F32),
         in_specs=[vmem] * len(operands),
         out_specs=vmem,
-        scratch_shapes=[VMEM((rows, width), BF16)] + [state] * 5,
-        compiler_params=pltpu.CompilerParams(vmem_limit_bytes=16 * MIB),
+        scratch_shapes=[VMEM((rows, width), BF16), state] + [VMEM((rows, TILE), F32)] * 2 + [state] * STATS,
+        compiler_params=pltpu.CompilerParams(vmem_limit_bytes=10 * MIB),
         cost_estimate=pl.CostEstimate(
             flops=2 * rows * width * vocab_dev,
             bytes_accessed=2 * width * vocab_dev,
@@ -225,15 +335,24 @@
 
 def shards(n_tok, n_voc, hidden, norm_gain, head_weight, lengths, offsets, slot_request, targets):
     req_dev, span, _ = hidden.shape
-    n_dev = n_tok * n_voc
+    n_dev, per_dev = n_tok * n_voc, req_dev * span
+    over_y = range(1, n_voc // RING)
+    cut = (head_weight.shape[1] // 256 + 1) // 2 * 256
     own = pack(hidden, norm_gain, lengths, offsets, slot_request, targets, n_voc)
-    side = n_voc // RING
-    steps = [(z, y) for z in range(RING) for y in range(side)]
-    steps.sort(key=lambda at: (min(at[0], RING - at[0]) + min(at[1], side - at[1]), at[0]))
-    blocks = [own] + [shift(own, z, y, n_voc) for z, y in steps[1:]]
-    half = len(blocks) // 2
-    sent = score(blocks[:half], head_weight, None, n_dev, req_dev * span)
-    sent = score(blocks[half:], head_weight, sent, n_dev, req_dev * span)
+    below = shift(own, -1, 0, n_voc)
+    beside = [shift(own, 0, y, n_voc) for y in over_y]
+    above = shift(own, 1, 0, n_voc)
+    sums, first = load([own], head_weight, None, 0, cut, n_dev, per_dev)
+    sums, below, beside, above, own = lax.optimization_barrier((sums, below, beside, above, own))
+    far = shift(below, -1, 0, n_voc)
+    corners = [shift(a, 1, 0, n_voc) for a in beside] + [shift(below, 0, y, n_voc) for y in over_y]
+    sent, second = load([own], head_weight, sums, cut, None, n_dev, per_dev)
+    sent, far = lax.optimization_barrier((sent, far))
+    farthest = [shift(far, 0, y, n_voc) for y in over_y]
+    weights = (first, second)
+    for blocks in ([below, *beside, above, far], [*corners, *farthest]):
+        for at in range(0, len(blocks), MOST):
+            sent = score(blocks[at : at + MOST], weights, sent, n_dev, per_dev)
     everything = lax.all_to_all(sent, ("tok", "voc"), 0, 0, tiled=True)
     return finish(everything, req_dev, span)
 

time: 75.8 us -> 53.7 us (0.71)
  local copies, waits for them, and re-layouts: 21.2 us -> 0 us
  Pallas kernels: 17.9 us -> 26.6 us
  waiting for transfers between devices: 8.7 us -> 2.37 us
  starting transfers between devices: 15.5 us -> 11.7 us
    unnamed x16 -> x0, local copies, waits for them, and re-layouts: 21.2 us -> none
    pallas_call x0 -> x2, Pallas kernels: none -> 11.9 us  [load(): pl.pallas_call(functools.partial(load_kernel, len(blocks), lo, None if la...]
    ppermute x7, waiting for transfers between devices: 8.7 us -> 2.37 us  [shift(): return lax.ppermute(block, 'voc', pairs)]
    ppermute x7, starting transfers between devices: 15.5 us -> 11.7 us  [shift(): return lax.ppermute(block, 'voc', pairs)]
    pallas_call x2, Pallas kernels: 16.3 us -> 12.6 us  [score(): pl.pallas_call(functools.partial(score_kernel, count, before is not None,...]
  transfers between devices with their start and end apart: 7 -> 7, of which waited for: 3 -> 1; matrix products, arithmetic and copies ran while one was open for 0% -> 0% of each run, Pallas kernels for 11% -> 36%
where the time goes in v2:
time: 53.7 us; the launch traced here: 53.6 us
  Pallas kernels  26.6 us (50%)
  blocking collectives  12.2 us (23%)
  starting transfers between devices  11.7 us (22%)
  waiting for transfers between devices  2.37 us (4%)
  between operations  0.69 us (1%)
    pallas_call x2, Pallas kernels, score(): pl.pallas_call(functools.partial(score_kernel, count, before is not None,...  12.6 us
    all_to_all x1, blocking collectives, shards(): everything = lax.all_to_all(sent, ('tok', 'voc'), 0, 0, tiled=True)  12.2 us
    pallas_call x2, Pallas kernels, load(): pl.pallas_call(functools.partial(load_kernel, len(blocks), lo, None if la...  11.9 us
    ppermute x7, starting transfers between devices, shift(): return lax.ppermute(block, 'voc', pairs)  11.7 us
    ppermute x7, waiting for transfers between devices, shift(): return lax.ppermute(block, 'voc', pairs)  2.37 us
    pallas_call x1, Pallas kernels, pack(): pl.pallas_call(functools.partial(pack_kernel, n_voc), out_shape=jax.Shape...  1.34 us
  transfers between devices with their start and end apart: 7, of which 1 were waited for; matrix products, arithmetic and copies ran while one was open for 0% of the time, Pallas kernels for 36%

profile of v2, /device:TPU:0, one launch (start us, length us, event | category | flops | bytes accessed | tf_op | source)
XLA Modules:
  0.0 53.6 jit_solution(11238994975824839357)
XLA Ops:
  0.6 1.3 %pack.1.refs_0_ = bf16[48,2176]{1,0:T(8,128)(2,1)S(1)} custom-call(s32[2]{0:T(128)} %refs_0_.1, s32[2]{0:T(128)} %refs_1_.3, s32[64]{0:T(128)} %refs_2_.1, bf16[2,32,2048]{2,1,0:T(8,128)(2,1)} %refs_3_.1, f32[1,2048]{1,0:T(1,128)} %bitcast.1, s32[2,32]{1,0:T(2,128)} %refs_5_.1), custom_call_target="tpu_custom_call" | custom-call | tf_op jit(solution)/shard_map/pack/pallas_call | solution.py:76
  2.0 5.1 %collective-permute-start = (bf16[48,2176]{1,0:T(8,128)(2,1)S(1)}, bf16[48,2176]{1,0:T(8,128)(2,1)S(1)}, u32[]{:S(2)}, u32[]{:S(2)}) collective-permute-start(bf16[48,2176]{1,0:T(8,128)(2,1)S(1)} %pack.1.refs_0_), channel_id=1, source_target_pairs={{0,6},{1,7},{2,0},{3,1},{4,2},{5,3},{6,4},{7,5},{8,14},{9,15},{10,... | collective-permute-start | bytes 626696 | tf_op jit(solution)/shard_map/ppermute | solution.py:333
  7.1 1.5 %collective-permute-start.1 = (bf16[48,2176]{1,0:T(8,128)(2,1)S(1)}, bf16[48,2176]{1,0:T(8,128)(2,1)S(1)}, u32[]{:S(2)}, u32[]{:S(2)}) collective-permute-start(bf16[48,2176]{1,0:T(8,128)(2,1)S(1)} %pack.1.refs_0_), channel_id=1, source_target_pairs={{0,1},{1,0},{2,3},{3,2},{4,5},{5,4},{6,7},{7,6},{8,9},{9,8},{10,11... | collective-permute-start | bytes 626696 | tf_op jit(solution)/shard_map/ppermute | solution.py:333
  8.6 0.0 collective-permute-start.2
  8.6 5.9 %load.2 = (f32[4,48,128]{2,1,0:T(8,128)S(1)}, bf16[2048,3328]{1,0:T(8,128)(2,1)S(1)}) custom-call(bf16[48,2176]{1,0:T(8,128)(2,1)S(1)} %pack.1.refs_0_, bf16[2048,6400]{1,0:T(8,128)(2,1)} %refs_1_.5), custom_call_target="tpu_custom_call" | custom-call | flops 654311424 | bytes 13631488 | tf_op jit(solution)/shard_map/load/pallas_call | solution.py:238
  14.5 0.0 collective-permute-done.refs_0_
  14.5 0.0 collective-permute-done.1.refs_1_
  14.6 2.3 %collective-permute-done.2.refs_2_ = bf16[48,2176]{1,0:T(8,128)(2,1)S(1)} collective-permute-done((bf16[48,2176]{1,0:T(8,128)(2,1)S(1)}, bf16[48,2176]{1,0:T(8,128)(2,1)S(1)}, u32[]{:S(2)}, u32[]{:S(2)}) %collective-permute-start.2) | collective-permute-done | bytes 208928 | tf_op jit(solution)/shard_map/ppermute | solution.py:333
  16.9 3.0 %collective-permute-start.5 = (bf16[48,2176]{1,0:T(8,128)(2,1)S(1)}, bf16[48,2176]{1,0:T(8,128)(2,1)S(1)}, u32[]{:S(2)}, u32[]{:S(2)}) collective-permute-start(bf16[48,2176]{1,0:T(8,128)(2,1)S(1)} %collective-permute-done.refs_0_), channel_id=1, source_target_pairs={{0,6},{1,7},{2,0},{3,1},{4,2},{5,3},{6,4},{7,5},{8,14},{9,15},{10,... | collective-permute-start | bytes 626696 | tf_op jit(solution)/shard_map/ppermute | solution.py:333
  19.9 0.5 collective-permute-start.4
  20.4 0.1 collective-permute-start.3
  20.4 6.0 %load.3 = (f32[32,4,128]{2,1,0:T(4,128)S(1)}, bf16[2048,3072]{1,0:T(8,128)(2,1)S(1)}) custom-call(bf16[48,2176]{1,0:T(8,128)(2,1)S(1)} %pack.1.refs_0_, bf16[2048,6400]{1,0:T(8,128)(2,1)} %refs_1_.5, f32[4,48,128]{2,1,0:T(8,128)S(1)} %get-tuple-element.17.refs_2_), custom_call_target="tpu_custom_call" | custom-call | flops 603979776 | bytes 12582912 | tf_op jit(solution)/shard_map/load/pallas_call | solution.py:238
  26.4 0.0 collective-permute-done.5.refs_3_
  26.4 1.5 %collective-permute-start.6 = (bf16[48,2176]{1,0:T(8,128)(2,1)S(1)}, bf16[48,2176]{1,0:T(8,128)(2,1)S(1)}, u32[]{:S(2)}, u32[]{:S(2)}) collective-permute-start(bf16[48,2176]{1,0:T(8,128)(2,1)S(1)} %collective-permute-done.5.refs_3_), channel_id=1, source_target_pairs={{0,1},{1,0},{2,3},{3,2},{4,5},{5,4},{6,7},{7,6},{8,9},{9,8},{10,11... | collective-permute-start | bytes 626696 | tf_op jit(solution)/shard_map/ppermute | solution.py:333
  28.0 7.1 %score.2.refs_5_ = f32[32,4,128]{2,1,0:T(4,128)S(1)} custom-call(bf16[48,2176]{1,0:T(8,128)(2,1)S(1)} %collective-permute-done.refs_0_, bf16[48,2176]{1,0:T(8,128)(2,1)S(1)} %collective-permute-done.1.refs_1_, bf16[48,2176]{1,0:T(8,128)(2,1)S(1)} %collective-permute-done.2.refs_2_, bf16[48,2176]{1,0:T(8,128)(2,1)S(1)} %collective-permute-done.5.refs_3_, ...), custom_call_target="tpu_custom_call" | custom-call | flops 5033164800 | bytes 26214400 | tf_op jit(solution)/shard_map/score/pallas_call | solution.py:277
  35.1 0.0 collective-permute-done.4.refs_1_
  35.1 0.0 collective-permute-done.3.refs_0_
  35.1 0.0 collective-permute-done.6.refs_2_
  35.1 5.5 %score.3 = f32[32,4,128]{2,1,0:T(4,128)S(1)} custom-call(bf16[48,2176]{1,0:T(8,128)(2,1)S(1)} %collective-permute-done.3.refs_0_, bf16[48,2176]{1,0:T(8,128)(2,1)S(1)} %collective-permute-done.4.refs_1_, bf16[48,2176]{1,0:T(8,128)(2,1)S(1)} %collective-permute-done.6.refs_2_, bf16[2048,3328]{1,0:T(8,128)(2,1)S(1)} %get-tuple-element.20.refs_4_.refs_3_, ...), custom_call_target="tpu_custom_call" | custom-call | flops 3774873600 | bytes 26214400 | tf_op jit(solution)/shard_map/score/pallas_call | solution.py:277
  40.6 12.2 %all_to_all.5.all_ref = f32[32,4,128]{2,1,0:T(4,128)S(1)} all-to-all(f32[32,4,128]{2,1,0:T(4,128)S(1)} %score.3), channel_id=1, replica_groups=mesh['tok'=4,'voc'=8] {'tok','voc'}, dimensions={0} | all-to-all | bytes 131072 | tf_op jit(solution)/shard_map/all_to_all | solution.py:356
  52.8 0.7 %finish.1 = (f32[2,32]{1,0:T(2,128)}, f32[2,32]{1,0:T(2,128)}) custom-call(f32[32,4,128]{2,1,0:T(4,128)S(1)} %all_to_all.5.all_ref), custom_call_target="tpu_custom_call" | custom-call | tf_op jit(solution)/shard_map/finish/pallas_call | solution.py:316
Async XLA Ops:
  2.0 12.6 %collective-permute-start = (bf16[48,2176]{1,0:T(8,128)(2,1)S(1)}, bf16[48,2176]{1,0:T(8,128)(2,1)S(1)}, u32[]{:S(2)}, u32[]{:S(2)}) collective-permute-start(bf16[48,2176]{1,0:T(8,128)(2,1)S(1)} %pack.1.refs_0_), channel_id=1, source_target_pairs={{0,6},{1,7},{2,0},{3,1},{4,2},{5,3},{6,4},{7,5},{8,14},{9,15},{10,... | collective-permute-start | bytes 626696 | tf_op jit(solution)/shard_map/ppermute | solution.py:333
  7.1 7.5 %collective-permute-start.1 = (bf16[48,2176]{1,0:T(8,128)(2,1)S(1)}, bf16[48,2176]{1,0:T(8,128)(2,1)S(1)}, u32[]{:S(2)}, u32[]{:S(2)}) collective-permute-start(bf16[48,2176]{1,0:T(8,128)(2,1)S(1)} %pack.1.refs_0_), channel_id=1, source_target_pairs={{0,1},{1,0},{2,3},{3,2},{4,5},{5,4},{6,7},{7,6},{8,9},{9,8},{10,11... | collective-permute-start | bytes 626696 | tf_op jit(solution)/shard_map/ppermute | solution.py:333
  8.6 8.3 %collective-permute-start.2 = (bf16[48,2176]{1,0:T(8,128)(2,1)S(1)}, bf16[48,2176]{1,0:T(8,128)(2,1)S(1)}, u32[]{:S(2)}, u32[]{:S(2)}) collective-permute-start(bf16[48,2176]{1,0:T(8,128)(2,1)S(1)} %pack.1.refs_0_), channel_id=1, source_target_pairs={{0,2},{1,3},{2,4},{3,5},{4,6},{5,7},{6,0},{7,1},{8,10},{9,11},{10,... | collective-permute-start | bytes 626696 | tf_op jit(solution)/shard_map/ppermute | solution.py:333
  16.9 9.5 %collective-permute-start.5 = (bf16[48,2176]{1,0:T(8,128)(2,1)S(1)}, bf16[48,2176]{1,0:T(8,128)(2,1)S(1)}, u32[]{:S(2)}, u32[]{:S(2)}) collective-permute-start(bf16[48,2176]{1,0:T(8,128)(2,1)S(1)} %collective-permute-done.refs_0_), channel_id=1, source_target_pairs={{0,6},{1,7},{2,0},{3,1},{4,2},{5,3},{6,4},{7,5},{8,14},{9,15},{10,... | collective-permute-start | bytes 626696 | tf_op jit(solution)/shard_map/ppermute | solution.py:333
  19.9 15.2 %collective-permute-start.4 = (bf16[48,2176]{1,0:T(8,128)(2,1)S(1)}, bf16[48,2176]{1,0:T(8,128)(2,1)S(1)}, u32[]{:S(2)}, u32[]{:S(2)}) collective-permute-start(bf16[48,2176]{1,0:T(8,128)(2,1)S(1)} %collective-permute-done.refs_0_), channel_id=1, source_target_pairs={{0,1},{1,0},{2,3},{3,2},{4,5},{5,4},{6,7},{7,6},{8,9},{9,8},{10,11... | collective-permute-start | bytes 626696 | tf_op jit(solution)/shard_map/ppermute | solution.py:333
  20.4 14.7 %collective-permute-start.3 = (bf16[48,2176]{1,0:T(8,128)(2,1)S(1)}, bf16[48,2176]{1,0:T(8,128)(2,1)S(1)}, u32[]{:S(2)}, u32[]{:S(2)}) collective-permute-start(bf16[48,2176]{1,0:T(8,128)(2,1)S(1)} %collective-permute-done.1.refs_1_), channel_id=1, source_target_pairs={{0,2},{1,3},{2,4},{3,5},{4,6},{5,7},{6,0},{7,1},{8,10},{9,11},{10,... | collective-permute-start | bytes 626696 | tf_op jit(solution)/shard_map/ppermute | solution.py:333
  26.4 8.7 %collective-permute-start.6 = (bf16[48,2176]{1,0:T(8,128)(2,1)S(1)}, bf16[48,2176]{1,0:T(8,128)(2,1)S(1)}, u32[]{:S(2)}, u32[]{:S(2)}) collective-permute-start(bf16[48,2176]{1,0:T(8,128)(2,1)S(1)} %collective-permute-done.5.refs_3_), channel_id=1, source_target_pairs={{0,1},{1,0},{2,3},{3,2},{4,5},{5,4},{6,7},{7,6},{8,9},{9,8},{10,11... | collective-permute-start | bytes 626696 | tf_op jit(solution)/shard_map/ppermute | solution.py:333

commit v3 on v2

--- a/solution.py
+++ b/solution.py
@@ -15,9 +15,9 @@
 NOWHERE = (1 << (2 * DIGIT)) - 1
 STATS = 4
 TILE = 1280
-PIECE = 512
-AHEAD = 4
 MOST = 4
+CUT = 2560
+PIECE = 1280
 F32 = jnp.float32
 BF16 = jnp.bfloat16
 VMEM = pltpu.VMEM
@@ -167,17 +167,18 @@
             out_ref[to, :, :per_dev] = part
 
 
-def sweep(x_ref, plan, logits, state, wanted, fresh):
+def sweep(x_ref, plan, logits, state, wanted):
     last = None
-    for at, (weight_ref, column, base, wide, wait) in enumerate(plan):
-        wait()
+    for at, (weight_ref, column, base, wide, copy) in enumerate(plan):
+        if copy is not None:
+            copy.wait()
         logits[at % 2][:, :wide] = jnp.dot(
             x_ref[...], weight_ref[:, column : column + wide], preferred_element_type=F32
         )
         if last is not None:
-            take(logits[(at - 1) % 2], state, wanted, *last, fresh and at == 1)
-        last = (base, wide)
-    take(logits[(len(plan) - 1) % 2], state, wanted, *last, fresh and len(plan) == 1)
+            take(*last)
+        last = logits[at % 2], state, wanted, base, wide, at == 0
+    take(*last)
 
 
 def wanted_columns(target, vocab_dev):
@@ -185,109 +186,106 @@
     return target - first - iota(target.shape, 1).astype(F32)
 
 
-def load_kernel(count, lo, hi, per_dev, *refs):
-    last = hi is None
-    blocks, (weight_ref, *refs) = refs[:count], refs[count:]
-    if last:
-        before_ref, out_ref, held_ref, *refs = refs
-    else:
-        state_ref, held_ref, *refs = refs
-    x_ref, place_ref, even_ref, odd_ref, sems, *refs = refs
-    vocab_dev = weight_ref.shape[1]
-    hi = vocab_dev if last else hi
-    plan = tiles(hi - lo, PIECE)
-    fetches = [
-        pltpu.make_async_copy(
+def fetch(weight_ref, held_ref, sems, lo):
+    started = []
+    for at, (base, wide) in enumerate(tiles(held_ref.shape[1], PIECE)):
+        copy = pltpu.make_async_copy(
             weight_ref.at[:, pl.ds(lo + base, wide)], held_ref.at[:, pl.ds(base, wide)], sems.at[at]
         )
-        for at, (base, wide) in enumerate(plan)
-    ]
-    for fetch in fetches[:AHEAD]:
-        fetch.start()
+        copy.start()
+        started.append((base, wide, copy))
+    return started
+
+
+def preload_kernel(after_ref, weight_ref, held_ref, sems):
+    for _, _, copy in fetch(weight_ref, held_ref, sems, 0):
+        copy.wait()
+
+
+def early_kernel(count, per_dev, *refs):
+    blocks, (first_ref, weight_ref, *refs) = refs[:count], refs[count:]
+    out_ref, held_ref, x_ref, place_ref, even_ref, odd_ref, sems, *state = refs
+    cut = first_ref.shape[1]
+    copies = fetch(weight_ref, held_ref, sems, cut)
     target = assemble(blocks, x_ref, place_ref)
-    state = refs if last else [state_ref.at[at] for at in range(STATS)]
-    if last:
-        for at in range(STATS):
-            state[at][...] = before_ref[at]
-
-    def arrival(at):
-        def wait():
-            fetches[at].wait()
-            if at + AHEAD < len(fetches):
-                fetches[at + AHEAD].start()
-
-        return wait
-
-    steps = [(held_ref, base, lo + base, wide, arrival(at)) for at, (base, wide) in enumerate(plan)]
-    sweep(x_ref, steps, (even_ref, odd_ref), state, wanted_columns(target, vocab_dev), not last)
-    if last:
-        route(state, place_ref, None, out_ref, per_dev)
-
-
-def load(blocks, weight, before, lo, hi, n_dev, per_dev):
-    rows, width = len(blocks) * blocks[0].shape[0], blocks[0].shape[1] - LANES
-    vocab_dev = weight.shape[1]
-    last = before is not None
-    count = (vocab_dev if last else hi) - lo
-    vmem = pl.BlockSpec(memory_space=VMEM)
-    result = (n_dev, STATS, LANES) if last else (STATS, rows, LANES)
-    operands = [pltpu.with_memory_space_constraint(a, VMEM) for a in blocks]
-    operands.append(pltpu.with_memory_space_constraint(weight, pltpu.HBM))
-    operands += [before] if last else []
-    state = VMEM((rows, LANES), F32)
-    return pl.pallas_call(
-        functools.partial(load_kernel, len(blocks), lo, None if last else hi, per_dev),
-        out_shape=(jax.ShapeDtypeStruct(result, F32), VMEM((width, count), BF16)),
-        in_specs=[vmem] * len(blocks) + [pl.BlockSpec(memory_space=pl.ANY)] + [vmem] * last,
-        out_specs=(vmem, vmem),
-        scratch_shapes=[VMEM((rows, width), BF16), state]
-        + [VMEM((rows, PIECE), F32)] * 2
-        + [pltpu.SemaphoreType.DMA((len(tiles(count, PIECE)),))]
-        + [state] * (STATS * last),
-        compiler_params=pltpu.CompilerParams(vmem_limit_bytes=6 * MIB),
-        cost_estimate=pl.CostEstimate(
-            flops=2 * rows * width * count, bytes_accessed=2 * width * count, transcendentals=rows * count
-        ),
-        name="load",
-    )(*operands)
-
-
-def score_kernel(count, carried, per_dev, *refs):
-    blocks, (first_ref, second_ref, *refs) = refs[:count], refs[count:]
-    if carried:
-        before_ref, *refs = refs
+    plan = [(first_ref, base, base, wide, None) for base, wide in tiles(cut, TILE)]
+    plan += [(held_ref, base, cut + base, wide, copy) for base, wide, copy in copies]
+    sweep(x_ref, plan, (even_ref, odd_ref), state, wanted_columns(target, weight_ref.shape[1]))
+    route(state, place_ref, None, out_ref, per_dev)
+
+
+def late_kernel(count, per_dev, *refs):
+    blocks, (first_ref, second_ref, before_ref, *refs) = refs[:count], refs[count:]
     out_ref, x_ref, place_ref, even_ref, odd_ref, *state = refs
     cut = first_ref.shape[1]
     target = assemble(blocks, x_ref, place_ref)
-    steps = [(first_ref, base, base, wide, lambda: None) for base, wide in tiles(cut, TILE)]
-    steps += [(second_ref, base, cut + base, wide, lambda: None) for base, wide in tiles(second_ref.shape[1], TILE)]
-    wanted = wanted_columns(target, cut + second_ref.shape[1])
-    sweep(x_ref, steps, (even_ref, odd_ref), state, wanted, True)
-    route(state, place_ref, before_ref if carried else None, out_ref, per_dev)
-
-
-def score(blocks, weights, before, n_dev, per_dev):
-    count = len(blocks)
-    rows, width = count * blocks[0].shape[0], blocks[0].shape[1] - LANES
-    vocab_dev = sum(a.shape[1] for a in weights)
-    vmem = pl.BlockSpec(memory_space=VMEM)
-    operands = [pltpu.with_memory_space_constraint(a, VMEM) for a in (*blocks, *weights)]
-    operands += [] if before is None else [before]
-    state = VMEM((rows, LANES), F32)
+    plan = [(first_ref, base, base, wide, None) for base, wide in tiles(cut, TILE)]
+    plan += [(second_ref, base, cut + base, wide, None) for base, wide in tiles(second_ref.shape[1], TILE)]
+    sweep(x_ref, plan, (even_ref, odd_ref), state, wanted_columns(target, cut + second_ref.shape[1]))
+    route(state, place_ref, before_ref, out_ref, per_dev)
+
+
+def call(kernel, name, operands, spaces, out_shape, rows, wide, scratch, columns):
+    specs = [pl.BlockSpec(memory_space=pl.ANY if space is pltpu.HBM else VMEM) for space in spaces]
+    operands = [
+        a if space is None else pltpu.with_memory_space_constraint(a, space) for a, space in zip(operands, spaces)
+    ]
+    width = operands[0].shape[1] - LANES
     return pl.pallas_call(
-        functools.partial(score_kernel, count, before is not None, per_dev),
-        out_shape=jax.ShapeDtypeStruct((n_dev, STATS, LANES), F32),
-        in_specs=[vmem] * len(operands),
-        out_specs=vmem,
-        scratch_shapes=[VMEM((rows, width), BF16), state] + [VMEM((rows, TILE), F32)] * 2 + [state] * STATS,
+        kernel,
+        out_shape=out_shape,
+        in_specs=specs,
+        out_specs=jax.tree.map(lambda _: pl.BlockSpec(memory_space=VMEM), out_shape),
+        scratch_shapes=[VMEM((rows, width), BF16), VMEM((rows, LANES), F32)] + [VMEM((rows, wide), F32)] * 2 + scratch,
         compiler_params=pltpu.CompilerParams(vmem_limit_bytes=10 * MIB),
         cost_estimate=pl.CostEstimate(
-            flops=2 * rows * width * vocab_dev,
-            bytes_accessed=2 * width * vocab_dev,
-            transcendentals=rows * vocab_dev,
+            flops=2 * rows * width * columns, bytes_accessed=2 * width * columns, transcendentals=rows * columns
         ),
-        name="score",
+        name=name,
     )(*operands)
+
+
+def preload(after, weight, cut):
+    return pl.pallas_call(
+        preload_kernel,
+        out_shape=VMEM((weight.shape[0], cut), BF16),
+        in_specs=[pl.BlockSpec(memory_space=pl.ANY)] * 2,
+        out_specs=pl.BlockSpec(memory_space=VMEM),
+        scratch_shapes=[pltpu.SemaphoreType.DMA((len(tiles(cut, PIECE)),))],
+        compiler_params=pltpu.CompilerParams(vmem_limit_bytes=MIB),
+        name="preload",
+    )(after, pltpu.with_memory_space_constraint(weight, pltpu.HBM))
+
+
+def early(blocks, first, weight, n_dev, per_dev):
+    rows = len(blocks) * blocks[0].shape[0]
+    rest = weight.shape[1] - first.shape[1]
+    return call(
+        functools.partial(early_kernel, len(blocks), per_dev),
+        "early",
+        (*blocks, first, weight),
+        (VMEM,) * (len(blocks) + 1) + (pltpu.HBM,),
+        (jax.ShapeDtypeStruct((n_dev, STATS, LANES), F32), VMEM((weight.shape[0], rest), BF16)),
+        rows,
+        TILE,
+        [pltpu.SemaphoreType.DMA((len(tiles(rest, PIECE)),))] + [VMEM((rows, LANES), F32)] * STATS,
+        weight.shape[1],
+    )
+
+
+def late(blocks, held, before, n_dev, per_dev):
+    rows = len(blocks) * blocks[0].shape[0]
+    return call(
+        functools.partial(late_kernel, len(blocks), per_dev),
+        "late",
+        (*blocks, *held, before),
+        (VMEM,) * (len(blocks) + 2) + (None,),
+        jax.ShapeDtypeStruct((n_dev, STATS, LANES), F32),
+        rows,
+        TILE,
+        [VMEM((rows, LANES), F32)] * STATS,
+        sum(a.shape[1] for a in held),
+    )
 
 
 def finish_kernel(all_ref, logprob_ref, entropy_ref):
@@ -337,22 +335,18 @@
     req_dev, span, _ = hidden.shape
     n_dev, per_dev = n_tok * n_voc, req_dev * span
     over_y = range(1, n_voc // RING)
-    cut = (head_weight.shape[1] // 256 + 1) // 2 * 256
     own = pack(hidden, norm_gain, lengths, offsets, slot_request, targets, n_voc)
     below = shift(own, -1, 0, n_voc)
     beside = [shift(own, 0, y, n_voc) for y in over_y]
     above = shift(own, 1, 0, n_voc)
-    sums, first = load([own], head_weight, None, 0, cut, n_dev, per_dev)
-    sums, below, beside, above, own = lax.optimization_barrier((sums, below, beside, above, own))
-    far = shift(below, -1, 0, n_voc)
-    corners = [shift(a, 1, 0, n_voc) for a in beside] + [shift(below, 0, y, n_voc) for y in over_y]
-    sent, second = load([own], head_weight, sums, cut, None, n_dev, per_dev)
-    sent, far = lax.optimization_barrier((sent, far))
-    farthest = [shift(far, 0, y, n_voc) for y in over_y]
-    weights = (first, second)
-    for blocks in ([below, *beside, above, far], [*corners, *farthest]):
-        for at in range(0, len(blocks), MOST):
-            sent = score(blocks[at : at + MOST], weights, sent, n_dev, per_dev)
+    left = preload(own, head_weight, CUT)
+    left, below = lax.optimization_barrier((left, below))
+    far = [shift(below, -1, y, n_voc) for y in range(n_voc // RING)]
+    corners = [shift(a, 0, y, n_voc) for y in over_y for a in (below, above)]
+    sent, right = early([own, below, *beside, above][:MOST], left, head_weight, n_dev, per_dev)
+    rest = [own, below, *beside, above][MOST:] + [*corners, *far]
+    for at in range(0, len(rest), MOST):
+        sent = late(rest[at : at + MOST], (left, right), sent, n_dev, per_dev)
     everything = lax.all_to_all(sent, ("tok", "voc"), 0, 0, tiled=True)
     return finish(everything, req_dev, span)
 

time: 53.7 us -> 48.3 us (0.90)
  Pallas kernels: 26.6 us -> 21.7 us
  starting transfers between devices: 11.7 us -> 13.8 us
  waiting for transfers between devices: 2.37 us -> 0.28 us
    pallas_call x4 -> x3, Pallas kernels: 24.5 us -> 19.6 us  [the longest x2 15.5 us: call(): pl.pallas_call(kernel, out_shape=out_shape, in_specs=specs, out_specs=jax...]
    ppermute x7, starting transfers between devices: 11.7 us -> 13.8 us  [shift(): return lax.ppermute(block, 'voc', pairs)]
    ppermute x7, waiting for transfers between devices: 2.37 us -> 0.28 us  [shift(): return lax.ppermute(block, 'voc', pairs)]
    all_to_all x1, blocking collectives: 12.2 us -> 11.7 us  [shards(): everything = lax.all_to_all(sent, ('tok', 'voc'), 0, 0, tiled=True)]
  transfers between devices with their start and end apart: 7 -> 7, of which waited for: 1 -> 1; matrix products, arithmetic and copies ran while one was open for 0% -> 0% of each run, Pallas kernels for 36% -> 26%
where the time goes in v3:
time: 48.3 us; the launch traced here: 48.1 us
  Pallas kernels  21.7 us (45%)
  starting transfers between devices  13.8 us (29%)
  blocking collectives  11.7 us (24%)
  between operations  0.69 us (1%)
    pallas_call x2, Pallas kernels, call(): pl.pallas_call(kernel, out_shape=out_shape, in_specs=specs, out_specs=jax...  15.5 us
    ppermute x7, starting transfers between devices, shift(): return lax.ppermute(block, 'voc', pairs)  13.8 us
    all_to_all x1, blocking collectives, shards(): everything = lax.all_to_all(sent, ('tok', 'voc'), 0, 0, tiled=True)  11.7 us
    pallas_call x1, Pallas kernels, preload(): pl.pallas_call(preload_kernel, out_shape=VMEM((weight.shape[0], cut), BF1...  4.09 us
    pallas_call x1, Pallas kernels, pack(): pl.pallas_call(functools.partial(pack_kernel, n_voc), out_shape=jax.Shape...  1.34 us
  transfers between devices with their start and end apart: 7, of which 1 were waited for; matrix products, arithmetic and copies ran while one was open for 0% of the time, Pallas kernels for 26%

profile of v3, /device:TPU:0, one launch (start us, length us, event | category | flops | bytes accessed | tf_op | source)
XLA Modules:
  0.0 48.1 jit_solution(9162546394501766793)
XLA Ops:
  0.6 1.3 %pack.1.after_ref.refs_0_ = bf16[48,2176]{1,0:T(8,128)(2,1)S(1)} custom-call(s32[2]{0:T(128)} %refs_0_.1, s32[2]{0:T(128)} %refs_1_.1, s32[64]{0:T(128)} %refs_2_.1, bf16[2,32,2048]{2,1,0:T(8,128)(2,1)} %refs_3_.1, f32[1,2048]{1,0:T(1,128)} %bitcast.1, s32[2,32]{1,0:T(2,128)} %refs_5_.2), custom_call_target="tpu_custom_call" | custom-call | tf_op jit(solution)/shard_map/pack/pallas_call | solution.py:76
  2.0 5.1 %collective-permute-start = (bf16[48,2176]{1,0:T(8,128)(2,1)S(1)}, bf16[48,2176]{1,0:T(8,128)(2,1)S(1)}, u32[]{:S(2)}, u32[]{:S(2)}) collective-permute-start(bf16[48,2176]{1,0:T(8,128)(2,1)S(1)} %pack.1.after_ref.refs_0_), channel_id=1, source_target_pairs={{0,6},{1,7},{2,0},{3,1},{4,2},{5,3},{6,4},{7,5},{8,14},{9,15},{10,... | collective-permute-start | bytes 626696 | tf_op jit(solution)/shard_map/ppermute | solution.py:331
  7.1 0.0 collective-permute-start.2
  7.1 1.5 %collective-permute-start.6 = (bf16[48,2176]{1,0:T(8,128)(2,1)S(1)}, bf16[48,2176]{1,0:T(8,128)(2,1)S(1)}, u32[]{:S(2)}, u32[]{:S(2)}) collective-permute-start(bf16[48,2176]{1,0:T(8,128)(2,1)S(1)} %pack.1.after_ref.refs_0_), channel_id=1, source_target_pairs={{0,1},{1,0},{2,3},{3,2},{4,5},{5,4},{6,7},{7,6},{8,9},{9,8},{10,11... | collective-permute-start | bytes 626696 | tf_op jit(solution)/shard_map/ppermute | solution.py:331
  8.6 4.1 %preload.1.refs_4_ = bf16[2048,2560]{1,0:T(8,128)(2,1)S(1)} custom-call(bf16[48,2176]{1,0:T(8,128)(2,1)S(1)} %pack.1.after_ref.refs_0_, bf16[2048,6400]{1,0:T(8,128)(2,1)} %refs_5_.3), custom_call_target="tpu_custom_call" | custom-call | tf_op jit(solution)/shard_map/preload/pallas_call | solution.py:249
  12.7 0.0 collective-permute-done.refs_1_
  12.7 1.5 %collective-permute-start.1 = (bf16[48,2176]{1,0:T(8,128)(2,1)S(1)}, bf16[48,2176]{1,0:T(8,128)(2,1)S(1)}, u32[]{:S(2)}, u32[]{:S(2)}) collective-permute-start(bf16[48,2176]{1,0:T(8,128)(2,1)S(1)} %collective-permute-done.refs_1_), channel_id=1, source_target_pairs={{0,1},{1,0},{2,3},{3,2},{4,5},{5,4},{6,7},{7,6},{8,9},{9,8},{10,11... | collective-permute-start | bytes 626696 | tf_op jit(solution)/shard_map/ppermute | solution.py:331
  14.2 4.3 %collective-permute-start.4 = (bf16[48,2176]{1,0:T(8,128)(2,1)S(1)}, bf16[48,2176]{1,0:T(8,128)(2,1)S(1)}, u32[]{:S(2)}, u32[]{:S(2)}) collective-permute-start(bf16[48,2176]{1,0:T(8,128)(2,1)S(1)} %collective-permute-done.refs_1_), channel_id=1, source_target_pairs={{0,6},{1,7},{2,0},{3,1},{4,2},{5,3},{6,4},{7,5},{8,14},{9,15},{10,... | collective-permute-start | bytes 626696 | tf_op jit(solution)/shard_map/ppermute | solution.py:331
  18.5 0.0 collective-permute-start.5
  18.5 0.0 collective-permute-done.2.refs_3_
  18.5 1.5 %collective-permute-start.3 = (bf16[48,2176]{1,0:T(8,128)(2,1)S(1)}, bf16[48,2176]{1,0:T(8,128)(2,1)S(1)}, u32[]{:S(2)}, u32[]{:S(2)}) collective-permute-start(bf16[48,2176]{1,0:T(8,128)(2,1)S(1)} %collective-permute-done.2.refs_3_), channel_id=1, source_target_pairs={{0,1},{1,0},{2,3},{3,2},{4,5},{5,4},{6,7},{7,6},{8,9},{9,8},{10,11... | collective-permute-start | bytes 626696 | tf_op jit(solution)/shard_map/ppermute | solution.py:331
  19.9 0.0 collective-permute-done.6.refs_2_
  19.9 8.5 %early.1 = (f32[32,4,128]{2,1,0:T(4,128)S(1)}, bf16[2048,3840]{1,0:T(8,128)(2,1)S(1)}) custom-call(bf16[48,2176]{1,0:T(8,128)(2,1)S(1)} %pack.1.after_ref.refs_0_, bf16[48,2176]{1,0:T(8,128)(2,1)S(1)} %collective-permute-done.refs_1_, bf16[48,2176]{1,0:T(8,128)(2,1)S(1)} %collective-permute-done.6.refs_2_, ...), custom_call_target="tpu_custom_call" | custom-call | flops 5033164800 | bytes 26214400 | tf_op jit(solution)/shard_map/early/pallas_call | solution.py:234
  28.4 0.0 collective-permute-done.1.refs_0_
  28.5 0.0 collective-permute-done.4.refs_2_
  28.5 0.0 collective-permute-done.5.refs_3_
  28.5 0.3 collective-permute-done.3.refs_1_
  28.7 7.0 %late.1 = f32[32,4,128]{2,1,0:T(4,128)S(1)} custom-call(bf16[48,2176]{1,0:T(8,128)(2,1)S(1)} %collective-permute-done.1.refs_0_, bf16[48,2176]{1,0:T(8,128)(2,1)S(1)} %collective-permute-done.3.refs_1_, bf16[48,2176]{1,0:T(8,128)(2,1)S(1)} %collective-permute-done.4.refs_2_, bf16[48,2176]{1,0:T(8,128)(2,1)S(1)} %collective-permute-done.5.refs_3_, ...), custom_call_target="tpu_custom_call" | custom-call | flops 5033164800 | bytes 26214400 | tf_op jit(solution)/shard_map/late/pallas_call | solution.py:234
  35.7 11.7 %all_to_all.5.all_ref = f32[32,4,128]{2,1,0:T(4,128)S(1)} all-to-all(f32[32,4,128]{2,1,0:T(4,128)S(1)} %late.1), channel_id=1, replica_groups=mesh['tok'=4,'voc'=8] {'tok','voc'}, dimensions={0} | all-to-all | bytes 131072 | tf_op jit(solution)/shard_map/all_to_all | solution.py:350
  47.4 0.7 %finish.1 = (f32[2,32]{1,0:T(2,128)}, f32[2,32]{1,0:T(2,128)}) custom-call(f32[32,4,128]{2,1,0:T(4,128)S(1)} %all_to_all.5.all_ref), custom_call_target="tpu_custom_call" | custom-call | tf_op jit(solution)/shard_map/finish/pallas_call | solution.py:314
Async XLA Ops:
  2.0 10.7 %collective-permute-start = (bf16[48,2176]{1,0:T(8,128)(2,1)S(1)}, bf16[48,2176]{1,0:T(8,128)(2,1)S(1)}, u32[]{:S(2)}, u32[]{:S(2)}) collective-permute-start(bf16[48,2176]{1,0:T(8,128)(2,1)S(1)} %pack.1.after_ref.refs_0_), channel_id=1, source_target_pairs={{0,6},{1,7},{2,0},{3,1},{4,2},{5,3},{6,4},{7,5},{8,14},{9,15},{10,... | collective-permute-start | bytes 626696 | tf_op jit(solution)/shard_map/ppermute | solution.py:331
  7.1 11.4 %collective-permute-start.2 = (bf16[48,2176]{1,0:T(8,128)(2,1)S(1)}, bf16[48,2176]{1,0:T(8,128)(2,1)S(1)}, u32[]{:S(2)}, u32[]{:S(2)}) collective-permute-start(bf16[48,2176]{1,0:T(8,128)(2,1)S(1)} %pack.1.after_ref.refs_0_), channel_id=1, source_target_pairs={{0,2},{1,3},{2,4},{3,5},{4,6},{5,7},{6,0},{7,1},{8,10},{9,11},{10,... | collective-permute-start | bytes 626696 | tf_op jit(solution)/shard_map/ppermute | solution.py:331
  7.1 12.8 %collective-permute-start.6 = (bf16[48,2176]{1,0:T(8,128)(2,1)S(1)}, bf16[48,2176]{1,0:T(8,128)(2,1)S(1)}, u32[]{:S(2)}, u32[]{:S(2)}) collective-permute-start(bf16[48,2176]{1,0:T(8,128)(2,1)S(1)} %pack.1.after_ref.refs_0_), channel_id=1, source_target_pairs={{0,1},{1,0},{2,3},{3,2},{4,5},{5,4},{6,7},{7,6},{8,9},{9,8},{10,11... | collective-permute-start | bytes 626696 | tf_op jit(solution)/shard_map/ppermute | solution.py:331
  12.7 15.7 %collective-permute-start.1 = (bf16[48,2176]{1,0:T(8,128)(2,1)S(1)}, bf16[48,2176]{1,0:T(8,128)(2,1)S(1)}, u32[]{:S(2)}, u32[]{:S(2)}) collective-permute-start(bf16[48,2176]{1,0:T(8,128)(2,1)S(1)} %collective-permute-done.refs_1_), channel_id=1, source_target_pairs={{0,1},{1,0},{2,3},{3,2},{4,5},{5,4},{6,7},{7,6},{8,9},{9,8},{10,11... | collective-permute-start | bytes 626696 | tf_op jit(solution)/shard_map/ppermute | solution.py:331
  14.2 14.3 %collective-permute-start.4 = (bf16[48,2176]{1,0:T(8,128)(2,1)S(1)}, bf16[48,2176]{1,0:T(8,128)(2,1)S(1)}, u32[]{:S(2)}, u32[]{:S(2)}) collective-permute-start(bf16[48,2176]{1,0:T(8,128)(2,1)S(1)} %collective-permute-done.refs_1_), channel_id=1, source_target_pairs={{0,6},{1,7},{2,0},{3,1},{4,2},{5,3},{6,4},{7,5},{8,14},{9,15},{10,... | collective-permute-start | bytes 626696 | tf_op jit(solution)/shard_map/ppermute | solution.py:331
  18.5 10.0 %collective-permute-start.5 = (bf16[48,2176]{1,0:T(8,128)(2,1)S(1)}, bf16[48,2176]{1,0:T(8,128)(2,1)S(1)}, u32[]{:S(2)}, u32[]{:S(2)}) collective-permute-start(bf16[48,2176]{1,0:T(8,128)(2,1)S(1)} %collective-permute-done.refs_1_), channel_id=1, source_target_pairs={{0,7},{1,6},{2,1},{3,0},{4,3},{5,2},{6,5},{7,4},{8,15},{9,14},{10,... | collective-permute-start | bytes 626696 | tf_op jit(solution)/shard_map/ppermute | solution.py:331
  18.5 10.3 %collective-permute-start.3 = (bf16[48,2176]{1,0:T(8,128)(2,1)S(1)}, bf16[48,2176]{1,0:T(8,128)(2,1)S(1)}, u32[]{:S(2)}, u32[]{:S(2)}) collective-permute-start(bf16[48,2176]{1,0:T(8,128)(2,1)S(1)} %collective-permute-done.2.refs_3_), channel_id=1, source_target_pairs={{0,1},{1,0},{2,3},{3,2},{4,5},{5,4},{6,7},{7,6},{8,9},{9,8},{10,11... | collective-permute-start | bytes 626696 | tf_op jit(solution)/shard_map/ppermute | solution.py:331

commit v4 on v3

--- a/solution.py
+++ b/solution.py
@@ -12,6 +12,7 @@
 RING = 4
 LANES = 128
 DIGIT = 7
+TAIL = 16
 NOWHERE = (1 << (2 * DIGIT)) - 1
 STATS = 4
 TILE = 1280
@@ -42,31 +43,36 @@
     values = hidden_ref[...].reshape(req_dev * span, width).astype(F32)
     square = jnp.mean(values * values, axis=-1, keepdims=True)
     normed = (values * lax.rsqrt(square + EPS) * gain_ref[...]).astype(BF16)
-    row = iota((rows, 1), 0)
-    source = jnp.zeros((rows, 1), jnp.int32)
-    place = jnp.zeros((rows, 1), jnp.int32)
-    target = jnp.zeros((rows, 1), F32)
-    for slot in range(req_dev):
-        step = row - slot * LIVE
-        mine = (step >= 0) & (step < LIVE)
-        position = offset_ref[slot] + step
-        source = jnp.where(mine, slot * span + position, source)
-        request = request_ref[device * req_dev + slot]
-        scored = jnp.where(step < length_ref[slot], request * span + position, NOWHERE)
-        place = jnp.where(mine, scored, place)
-        found = mine & (iota((rows, span), 1) == position)
-        ids = target_ref[slot : slot + 1, :].astype(F32)
-        target += jnp.sum(jnp.where(found, ids, 0.0), axis=1, keepdims=True)
+
+    def window(row):
+        source = place = jnp.zeros(row.shape, jnp.int32) + NOWHERE
+        for slot in range(req_dev):
+            step = row - slot * LIVE
+            mine = (step >= 0) & (step < LIVE)
+            position = offset_ref[slot] + step
+            request = request_ref[device * req_dev + slot]
+            source = jnp.where(mine, slot * span + position, source)
+            place = jnp.where(mine & (step < length_ref[slot]), request * span + position, place)
+        return source, place
+
+    source, _ = window(iota((rows, 1), 0))
     taken = (iota((rows, req_dev * span), 1) == source).astype(BF16)
-    out_ref[:, :width] = jnp.dot(taken, normed, preferred_element_type=F32).astype(BF16)
-    target = target.astype(jnp.int32)
+    sent = jnp.dot(taken, normed, preferred_element_type=F32).astype(BF16)
+    for at in range(width // LANES):
+        out_ref[at * rows : (at + 1) * rows, :] = sent[:, at * LANES : (at + 1) * LANES]
+    source, place = window(iota((1, LANES), 1))
+    taken = (iota((req_dev * span, LANES), 0) == source).astype(BF16)
+    target = jnp.concatenate([target_ref[slot : slot + 1, :] for slot in range(req_dev)], axis=1)
     low = (1 << DIGIT) - 1
-    digits = (target >> (2 * DIGIT), (target >> DIGIT) & low, target & low, place >> DIGIT, place & low)
-    lane = iota((rows, LANES), 1)
-    tail = jnp.zeros((rows, LANES), jnp.int32)
-    for at, digit in enumerate(digits):
-        tail = jnp.where(lane == at, digit, tail)
-    out_ref[:, width:] = tail.astype(F32).astype(BF16)
+    kind = iota((TAIL, req_dev * span), 0)
+    digits = jnp.zeros((TAIL, req_dev * span), jnp.int32)
+    for at, digit in enumerate((target >> (2 * DIGIT), (target >> DIGIT) & low, target & low)):
+        digits = jnp.where(kind == at, digit, digits)
+    tail = jnp.dot(digits.astype(F32).astype(BF16), taken, preferred_element_type=F32)
+    kind = iota((TAIL, LANES), 0)
+    for at, digit in enumerate((place >> DIGIT, place & low)):
+        tail = jnp.where(kind == at + 3, digit.astype(F32), tail)
+    out_ref[width // LANES * rows :, :] = tail.astype(BF16)
 
 
 def pack(hidden, norm_gain, lengths, offsets, slot_request, targets, n_voc):
@@ -75,7 +81,7 @@
     spaces = (pltpu.SMEM,) * 3 + (VMEM,) * 3
     return pl.pallas_call(
         functools.partial(pack_kernel, n_voc),
-        out_shape=jax.ShapeDtypeStruct((req_dev * LIVE, width + LANES), BF16),
+        out_shape=jax.ShapeDtypeStruct((width // LANES * req_dev * LIVE + TAIL, LANES), BF16),
         in_specs=[pl.BlockSpec(memory_space=pl.ANY)] * 6,
         out_specs=pl.BlockSpec(memory_space=VMEM),
         scratch_shapes=[space(a.shape, a.dtype) for space, a in zip(spaces, arrays)]
@@ -86,14 +92,11 @@
 
 
 def decode(tail):
-    at, column = iota((LANES, 2 * LANES), 0), iota((LANES, 2 * LANES), 1)
-    first = column < LANES
-    scale = jnp.zeros((LANES, 2 * LANES), F32)
-    for row, value in enumerate((1 << (2 * DIGIT), 1 << DIGIT, 1)):
-        scale = jnp.where(first & (at == row), float(value), scale)
-    for row, value in enumerate((1 << DIGIT, 1)):
-        scale = jnp.where((~first) & (at == row + 3), float(value), scale)
-    both = jnp.dot(tail, scale.astype(BF16), preferred_element_type=F32)
+    at, column = iota((TAIL, 2 * LANES), 0), iota((TAIL, 2 * LANES), 1)
+    scale = jnp.zeros((TAIL, 2 * LANES), F32)
+    for row, value in enumerate((1 << (2 * DIGIT), 1 << DIGIT, 1, 1 << DIGIT, 1)):
+        scale = jnp.where((at == row) & ((column < LANES) == (row < 3)), float(value), scale)
+    both = lax.dot_general(tail, scale.astype(BF16), (((0,), (0,)), ((), ())), preferred_element_type=F32)
     return both[:, :LANES], both[:, LANES:]
 
 
@@ -101,13 +104,22 @@
     return [(base, min(size, columns - base)) for base in range(0, columns, size)]
 
 
+def height(block, width):
+    return (block.shape[0] - TAIL) * LANES // width
+
+
 def assemble(blocks, x_ref, place_ref):
-    size, width = blocks[0].shape[0], x_ref.shape[1]
+    width = x_ref.shape[1]
+    size = height(blocks[0], width)
+    targets = []
     for at, block in enumerate(blocks):
-        x_ref[at * size : (at + 1) * size, :] = block[:, :width]
-    target, place = decode(jnp.concatenate([block[:, width:] for block in blocks], axis=0))
-    place_ref[...] = place
-    return target
+        rows = slice(at * size, (at + 1) * size)
+        for part in range(width // LANES):
+            x_ref[rows, part * LANES : (part + 1) * LANES] = block[part * size : (part + 1) * size, :]
+        target, place = decode(block[width // LANES * size :, :])
+        place_ref[rows, :] = place[:size]
+        targets.append(target[:size])
+    return jnp.concatenate(targets, axis=0)
 
 
 def take(logits_ref, state, wanted, base, wide, fresh):
@@ -225,18 +237,17 @@
     route(state, place_ref, before_ref, out_ref, per_dev)
 
 
-def call(kernel, name, operands, spaces, out_shape, rows, wide, scratch, columns):
+def call(kernel, name, operands, spaces, out_shape, rows, width, scratch, columns):
     specs = [pl.BlockSpec(memory_space=pl.ANY if space is pltpu.HBM else VMEM) for space in spaces]
     operands = [
         a if space is None else pltpu.with_memory_space_constraint(a, space) for a, space in zip(operands, spaces)
     ]
-    width = operands[0].shape[1] - LANES
     return pl.pallas_call(
         kernel,
         out_shape=out_shape,
         in_specs=specs,
         out_specs=jax.tree.map(lambda _: pl.BlockSpec(memory_space=VMEM), out_shape),
-        scratch_shapes=[VMEM((rows, width), BF16), VMEM((rows, LANES), F32)] + [VMEM((rows, wide), F32)] * 2 + scratch,
+        scratch_shapes=[VMEM((rows, width), BF16), VMEM((rows, LANES), F32)] + [VMEM((rows, TILE), F32)] * 2 + scratch,
         compiler_params=pltpu.CompilerParams(vmem_limit_bytes=10 * MIB),
         cost_estimate=pl.CostEstimate(
             flops=2 * rows * width * columns, bytes_accessed=2 * width * columns, transcendentals=rows * columns
@@ -258,23 +269,25 @@
 
 
 def early(blocks, first, weight, n_dev, per_dev):
-    rows = len(blocks) * blocks[0].shape[0]
+    width = weight.shape[0]
+    rows = len(blocks) * height(blocks[0], width)
     rest = weight.shape[1] - first.shape[1]
     return call(
         functools.partial(early_kernel, len(blocks), per_dev),
         "early",
         (*blocks, first, weight),
         (VMEM,) * (len(blocks) + 1) + (pltpu.HBM,),
-        (jax.ShapeDtypeStruct((n_dev, STATS, LANES), F32), VMEM((weight.shape[0], rest), BF16)),
+        (jax.ShapeDtypeStruct((n_dev, STATS, LANES), F32), VMEM((width, rest), BF16)),
         rows,
-        TILE,
+        width,
         [pltpu.SemaphoreType.DMA((len(tiles(rest, PIECE)),))] + [VMEM((rows, LANES), F32)] * STATS,
         weight.shape[1],
     )
 
 
 def late(blocks, held, before, n_dev, per_dev):
-    rows = len(blocks) * blocks[0].shape[0]
+    width = held[0].shape[0]
+    rows = len(blocks) * height(blocks[0], width)
     return call(
         functools.partial(late_kernel, len(blocks), per_dev),
         "late",
@@ -282,7 +295,7 @@
         (VMEM,) * (len(blocks) + 2) + (None,),
         jax.ShapeDtypeStruct((n_dev, STATS, LANES), F32),
         rows,
-        TILE,
+        width,
         [VMEM((rows, LANES), F32)] * STATS,
         sum(a.shape[1] for a in held),
     )

time: 48.3 us -> 47.6 us (0.986)
  blocking collectives: 11.7 us -> 10.9 us
  Pallas kernels: 21.7 us -> 22.2 us
    all_to_all x1, blocking collectives: 11.7 us -> 10.9 us  [shards(): everything = lax.all_to_all(sent, ('tok', 'voc'), 0, 0, tiled=True)]
    pallas_call x2, Pallas kernels: 15.5 us -> 16 us  [call(): pl.pallas_call(kernel, out_shape=out_shape, in_specs=specs, out_specs=jax...]
  transfers between devices with their start and end apart: 7 -> 7, of which waited for: 1 -> 0; matrix products, arithmetic and copies ran while one was open for 0% -> 0% of each run, Pallas kernels for 26% -> 27%
where the time goes in v4:
time: 47.6 us; the launch traced here: 47.4 us
  Pallas kernels  22.2 us (47%)
  starting transfers between devices  13.7 us (29%)
  blocking collectives  10.9 us (23%)
  between operations  0.7 us (1%)
    pallas_call x2, Pallas kernels, call(): pl.pallas_call(kernel, out_shape=out_shape, in_specs=specs, out_specs=jax...  16 us
    ppermute x7, starting transfers between devices, shift(): return lax.ppermute(block, 'voc', pairs)  13.7 us
    all_to_all x1, blocking collectives, shards(): everything = lax.all_to_all(sent, ('tok', 'voc'), 0, 0, tiled=True)  10.9 us
    pallas_call x1, Pallas kernels, preload(): pl.pallas_call(preload_kernel, out_shape=VMEM((weight.shape[0], cut), BF1...  4.09 us
    pallas_call x1, Pallas kernels, pack(): pl.pallas_call(functools.partial(pack_kernel, n_voc), out_shape=jax.Shape...  1.34 us
  transfers between devices with their start and end apart: 7, of which 0 were waited for; matrix products, arithmetic and copies ran while one was open for 0% of the time, Pallas kernels for 27%

profile of v4, /device:TPU:0, one launch (start us, length us, event | category | flops | bytes accessed | tf_op | source)
XLA Modules:
  0.0 47.4 jit_solution(6906385752851779879)
XLA Ops:
  0.6 1.3 %pack.1.after_ref.refs_0_ = bf16[784,128]{1,0:T(8,128)(2,1)S(1)} custom-call(s32[2]{0:T(128)} %refs_0_.1, s32[2]{0:T(128)} %refs_1_.1, s32[64]{0:T(128)} %refs_2_.1, bf16[2,32,2048]{2,1,0:T(8,128)(2,1)} %refs_3_.1, f32[1,2048]{1,0:T(1,128)} %bitcast.1, s32[2,32]{1,0:T(2,128)} %refs_5_.2), custom_call_target="tpu_custom_call" | custom-call | tf_op jit(solution)/shard_map/pack/pallas_call | solution.py:82
  2.0 5.1 %collective-permute-start = (bf16[784,128]{1,0:T(8,128)(2,1)S(1)}, bf16[784,128]{1,0:T(8,128)(2,1)S(1)}, u32[]{:S(2)}, u32[]{:S(2)}) collective-permute-start(bf16[784,128]{1,0:T(8,128)(2,1)S(1)} %pack.1.after_ref.refs_0_), channel_id=1, source_target_pairs={{0,6},{1,7},{2,0},{3,1},{4,2},{5,3},{6,4},{7,5},{8,14},{9,15},{10,... | collective-permute-start | bytes 602120 | tf_op jit(solution)/shard_map/ppermute | solution.py:344
  7.1 0.0 collective-permute-start.2
  7.1 1.5 %collective-permute-start.6 = (bf16[784,128]{1,0:T(8,128)(2,1)S(1)}, bf16[784,128]{1,0:T(8,128)(2,1)S(1)}, u32[]{:S(2)}, u32[]{:S(2)}) collective-permute-start(bf16[784,128]{1,0:T(8,128)(2,1)S(1)} %pack.1.after_ref.refs_0_), channel_id=1, source_target_pairs={{0,1},{1,0},{2,3},{3,2},{4,5},{5,4},{6,7},{7,6},{8,9},{9,8},{10,11... | collective-permute-start | bytes 602120 | tf_op jit(solution)/shard_map/ppermute | solution.py:344
  8.6 4.1 %preload.1.refs_4_ = bf16[2048,2560]{1,0:T(8,128)(2,1)S(1)} custom-call(bf16[784,128]{1,0:T(8,128)(2,1)S(1)} %pack.1.after_ref.refs_0_, bf16[2048,6400]{1,0:T(8,128)(2,1)} %refs_5_.3), custom_call_target="tpu_custom_call" | custom-call | tf_op jit(solution)/shard_map/preload/pallas_call | solution.py:260
  12.7 0.0 collective-permute-done.refs_1_
  12.7 1.3 %collective-permute-start.1 = (bf16[784,128]{1,0:T(8,128)(2,1)S(1)}, bf16[784,128]{1,0:T(8,128)(2,1)S(1)}, u32[]{:S(2)}, u32[]{:S(2)}) collective-permute-start(bf16[784,128]{1,0:T(8,128)(2,1)S(1)} %collective-permute-done.refs_1_), channel_id=1, source_target_pairs={{0,1},{1,0},{2,3},{3,2},{4,5},{5,4},{6,7},{7,6},{8,9},{9,8},{10,11... | collective-permute-start | bytes 602120 | tf_op jit(solution)/shard_map/ppermute | solution.py:344
  14.0 4.3 %collective-permute-start.4 = (bf16[784,128]{1,0:T(8,128)(2,1)S(1)}, bf16[784,128]{1,0:T(8,128)(2,1)S(1)}, u32[]{:S(2)}, u32[]{:S(2)}) collective-permute-start(bf16[784,128]{1,0:T(8,128)(2,1)S(1)} %collective-permute-done.refs_1_), channel_id=1, source_target_pairs={{0,6},{1,7},{2,0},{3,1},{4,2},{5,3},{6,4},{7,5},{8,14},{9,15},{10,... | collective-permute-start | bytes 602120 | tf_op jit(solution)/shard_map/ppermute | solution.py:344
  18.3 0.0 collective-permute-start.5
  18.3 0.0 collective-permute-done.2.refs_3_
  18.3 1.5 %collective-permute-start.3 = (bf16[784,128]{1,0:T(8,128)(2,1)S(1)}, bf16[784,128]{1,0:T(8,128)(2,1)S(1)}, u32[]{:S(2)}, u32[]{:S(2)}) collective-permute-start(bf16[784,128]{1,0:T(8,128)(2,1)S(1)} %collective-permute-done.2.refs_3_), channel_id=1, source_target_pairs={{0,1},{1,0},{2,3},{3,2},{4,5},{5,4},{6,7},{7,6},{8,9},{9,8},{10,11... | collective-permute-start | bytes 602120 | tf_op jit(solution)/shard_map/ppermute | solution.py:344
  19.8 0.0 collective-permute-done.6.refs_2_
  19.8 8.9 %early.1 = (f32[32,4,128]{2,1,0:T(4,128)S(1)}, bf16[2048,3840]{1,0:T(8,128)(2,1)S(1)}) custom-call(bf16[784,128]{1,0:T(8,128)(2,1)S(1)} %pack.1.after_ref.refs_0_, bf16[784,128]{1,0:T(8,128)(2,1)S(1)} %collective-permute-done.refs_1_, bf16[784,128]{1,0:T(8,128)(2,1)S(1)} %collective-permute-done.6.refs_2_, ...), custom_call_target="tpu_custom_call" | custom-call | flops 5033164800 | bytes 26214400 | tf_op jit(solution)/shard_map/early/pallas_call | solution.py:245
  28.7 0.0 collective-permute-done.1.refs_0_
  28.7 0.0 collective-permute-done.4.refs_2_
  28.7 0.0 collective-permute-done.5.refs_3_
  28.7 0.0 collective-permute-done.3.refs_1_
  28.7 7.1 %late.1 = f32[32,4,128]{2,1,0:T(4,128)S(1)} custom-call(bf16[784,128]{1,0:T(8,128)(2,1)S(1)} %collective-permute-done.1.refs_0_, bf16[784,128]{1,0:T(8,128)(2,1)S(1)} %collective-permute-done.3.refs_1_, bf16[784,128]{1,0:T(8,128)(2,1)S(1)} %collective-permute-done.4.refs_2_, bf16[784,128]{1,0:T(8,128)(2,1)S(1)} %collective-permute-done.5.refs_3_, ...), custom_call_target="tpu_custom_call" | custom-call | flops 5033164800 | bytes 26214400 | tf_op jit(solution)/shard_map/late/pallas_call | solution.py:245
  35.8 10.9 %all_to_all.5.all_ref = f32[32,4,128]{2,1,0:T(4,128)S(1)} all-to-all(f32[32,4,128]{2,1,0:T(4,128)S(1)} %late.1), channel_id=1, replica_groups=mesh['tok'=4,'voc'=8] {'tok','voc'}, dimensions={0} | all-to-all | bytes 131072 | tf_op jit(solution)/shard_map/all_to_all | solution.py:363
  46.7 0.7 %finish.1 = (f32[2,32]{1,0:T(2,128)}, f32[2,32]{1,0:T(2,128)}) custom-call(f32[32,4,128]{2,1,0:T(4,128)S(1)} %all_to_all.5.all_ref), custom_call_target="tpu_custom_call" | custom-call | tf_op jit(solution)/shard_map/finish/pallas_call | solution.py:327
Async XLA Ops:
  2.0 10.7 %collective-permute-start = (bf16[784,128]{1,0:T(8,128)(2,1)S(1)}, bf16[784,128]{1,0:T(8,128)(2,1)S(1)}, u32[]{:S(2)}, u32[]{:S(2)}) collective-permute-start(bf16[784,128]{1,0:T(8,128)(2,1)S(1)} %pack.1.after_ref.refs_0_), channel_id=1, source_target_pairs={{0,6},{1,7},{2,0},{3,1},{4,2},{5,3},{6,4},{7,5},{8,14},{9,15},{10,... | collective-permute-start | bytes 602120 | tf_op jit(solution)/shard_map/ppermute | solution.py:344
  7.1 11.2 %collective-permute-start.2 = (bf16[784,128]{1,0:T(8,128)(2,1)S(1)}, bf16[784,128]{1,0:T(8,128)(2,1)S(1)}, u32[]{:S(2)}, u32[]{:S(2)}) collective-permute-start(bf16[784,128]{1,0:T(8,128)(2,1)S(1)} %pack.1.after_ref.refs_0_), channel_id=1, source_target_pairs={{0,2},{1,3},{2,4},{3,5},{4,6},{5,7},{6,0},{7,1},{8,10},{9,11},{10,... | collective-permute-start | bytes 602120 | tf_op jit(solution)/shard_map/ppermute | solution.py:344
  7.1 12.7 %collective-permute-start.6 = (bf16[784,128]{1,0:T(8,128)(2,1)S(1)}, bf16[784,128]{1,0:T(8,128)(2,1)S(1)}, u32[]{:S(2)}, u32[]{:S(2)}) collective-permute-start(bf16[784,128]{1,0:T(8,128)(2,1)S(1)} %pack.1.after_ref.refs_0_), channel_id=1, source_target_pairs={{0,1},{1,0},{2,3},{3,2},{4,5},{5,4},{6,7},{7,6},{8,9},{9,8},{10,11... | collective-permute-start | bytes 602120 | tf_op jit(solution)/shard_map/ppermute | solution.py:344
  12.7 16.0 %collective-permute-start.1 = (bf16[784,128]{1,0:T(8,128)(2,1)S(1)}, bf16[784,128]{1,0:T(8,128)(2,1)S(1)}, u32[]{:S(2)}, u32[]{:S(2)}) collective-permute-start(bf16[784,128]{1,0:T(8,128)(2,1)S(1)} %collective-permute-done.refs_1_), channel_id=1, source_target_pairs={{0,1},{1,0},{2,3},{3,2},{4,5},{5,4},{6,7},{7,6},{8,9},{9,8},{10,11... | collective-permute-start | bytes 602120 | tf_op jit(solution)/shard_map/ppermute | solution.py:344
  14.0 14.7 %collective-permute-start.4 = (bf16[784,128]{1,0:T(8,128)(2,1)S(1)}, bf16[784,128]{1,0:T(8,128)(2,1)S(1)}, u32[]{:S(2)}, u32[]{:S(2)}) collective-permute-start(bf16[784,128]{1,0:T(8,128)(2,1)S(1)} %collective-permute-done.refs_1_), channel_id=1, source_target_pairs={{0,6},{1,7},{2,0},{3,1},{4,2},{5,3},{6,4},{7,5},{8,14},{9,15},{10,... | collective-permute-start | bytes 602120 | tf_op jit(solution)/shard_map/ppermute | solution.py:344
  18.3 10.4 %collective-permute-start.5 = (bf16[784,128]{1,0:T(8,128)(2,1)S(1)}, bf16[784,128]{1,0:T(8,128)(2,1)S(1)}, u32[]{:S(2)}, u32[]{:S(2)}) collective-permute-start(bf16[784,128]{1,0:T(8,128)(2,1)S(1)} %collective-permute-done.refs_1_), channel_id=1, source_target_pairs={{0,7},{1,6},{2,1},{3,0},{4,3},{5,2},{6,5},{7,4},{8,15},{9,14},{10,... | collective-permute-start | bytes 602120 | tf_op jit(solution)/shard_map/ppermute | solution.py:344
  18.3 10.4 %collective-permute-start.3 = (bf16[784,128]{1,0:T(8,128)(2,1)S(1)}, bf16[784,128]{1,0:T(8,128)(2,1)S(1)}, u32[]{:S(2)}, u32[]{:S(2)}) collective-permute-start(bf16[784,128]{1,0:T(8,128)(2,1)S(1)} %collective-permute-done.2.refs_3_), channel_id=1, source_target_pairs={{0,1},{1,0},{2,3},{3,2},{4,5},{5,4},{6,7},{7,6},{8,9},{9,8},{10,11... | collective-permute-start | bytes 602120 | tf_op jit(solution)/shard_map/ppermute | solution.py:344

commit v5 on v4

--- a/solution.py
+++ b/solution.py
@@ -16,6 +16,7 @@
 NOWHERE = (1 << (2 * DIGIT)) - 1
 STATS = 4
 TILE = 1280
+SHORT = 512
 MOST = 4
 CUT = 2560
 PIECE = 1280
@@ -102,6 +103,13 @@
 
 def tiles(columns, size):
     return [(base, min(size, columns - base)) for base in range(0, columns, size)]
+
+
+def shorten(plan):
+    *plan, (weight_ref, column, base, wide, copy) = plan
+    cut = max(wide - SHORT, 0)
+    head = [(weight_ref, column, base, cut, copy)] if cut else []
+    return plan + head + [(weight_ref, column + cut, base + cut, wide - cut, None if cut else copy)]
 
 
 def height(block, width):
@@ -149,9 +157,10 @@
     pick_ref[...] = pick
 
 
-def route(state, place_ref, before_ref, out_ref, per_dev):
+def route(state, place_ref, before_ref, out_ref, span, per_dev):
     peak_ref, sum_ref, dot_ref, pick_ref = state
     rows = place_ref.shape[0]
+    shift = span.bit_length() - 1
     lane = iota((rows, LANES), 1).astype(F32)
     peak = jnp.max(peak_ref[...], axis=1, keepdims=True)
     drop = peak_ref[...] - peak
@@ -167,13 +176,22 @@
         for part, piece in enumerate((high, middle, low)):
             stats = jnp.where(lane == float(8 * part + at), piece, stats)
     stats = stats.T.astype(BF16)[:32]
+    lane = iota((STATS, LANES), 1)
+    slots = []
+    for first_row in range(0, rows, LIVE):
+        request = jnp.broadcast_to(place_ref[first_row : first_row + 1, :].astype(jnp.int32) >> shift, (STATS, LANES))
+        spot = (request * span + (lane & (span - 1))).astype(F32)[:1]
+        there = (place_ref[...] == spot).astype(F32).astype(BF16)
+        moved = jnp.dot(stats, there, preferred_element_type=F32)
+        slots.append((request, (moved[0:8] + moved[8:16] + moved[16:24])[:STATS]))
     for group in range(out_ref.shape[0] * per_dev // LANES):
-        there = (place_ref[...] == lane + float(group * LANES)).astype(F32).astype(BF16)
-        moved = jnp.dot(stats, there, preferred_element_type=F32)
-        moved = (moved[0:8] + moved[8:16] + moved[16:24])[:STATS]
+        held = group * (LANES // span) + (lane >> shift)
+        total = jnp.zeros((STATS, LANES), F32)
+        for request, moved in slots:
+            total = jnp.where(request == held, moved, total)
         for at in range(LANES // per_dev):
             to = group * (LANES // per_dev) + at
-            part = moved[:, at * per_dev : (at + 1) * per_dev]
+            part = total[:, at * per_dev : (at + 1) * per_dev]
             if before_ref is not None:
                 part += before_ref[to, :, :per_dev]
             out_ref[to, :, :per_dev] = part
@@ -214,7 +232,7 @@
         copy.wait()
 
 
-def early_kernel(count, per_dev, *refs):
+def early_kernel(count, span, per_dev, *refs):
     blocks, (first_ref, weight_ref, *refs) = refs[:count], refs[count:]
     out_ref, held_ref, x_ref, place_ref, even_ref, odd_ref, sems, *state = refs
     cut = first_ref.shape[1]
@@ -222,19 +240,19 @@
     target = assemble(blocks, x_ref, place_ref)
     plan = [(first_ref, base, base, wide, None) for base, wide in tiles(cut, TILE)]
     plan += [(held_ref, base, cut + base, wide, copy) for base, wide, copy in copies]
-    sweep(x_ref, plan, (even_ref, odd_ref), state, wanted_columns(target, weight_ref.shape[1]))
-    route(state, place_ref, None, out_ref, per_dev)
-
-
-def late_kernel(count, per_dev, *refs):
+    sweep(x_ref, shorten(plan), (even_ref, odd_ref), state, wanted_columns(target, weight_ref.shape[1]))
+    route(state, place_ref, None, out_ref, span, per_dev)
+
+
+def late_kernel(count, span, per_dev, *refs):
     blocks, (first_ref, second_ref, before_ref, *refs) = refs[:count], refs[count:]
     out_ref, x_ref, place_ref, even_ref, odd_ref, *state = refs
     cut = first_ref.shape[1]
     target = assemble(blocks, x_ref, place_ref)
     plan = [(first_ref, base, base, wide, None) for base, wide in tiles(cut, TILE)]
     plan += [(second_ref, base, cut + base, wide, None) for base, wide in tiles(second_ref.shape[1], TILE)]
-    sweep(x_ref, plan, (even_ref, odd_ref), state, wanted_columns(target, cut + second_ref.shape[1]))
-    route(state, place_ref, before_ref, out_ref, per_dev)
+    sweep(x_ref, shorten(plan), (even_ref, odd_ref), state, wanted_columns(target, cut + second_ref.shape[1]))
+    route(state, place_ref, before_ref, out_ref, span, per_dev)
 
 
 def call(kernel, name, operands, spaces, out_shape, rows, width, scratch, columns):
@@ -268,12 +286,12 @@
     )(after, pltpu.with_memory_space_constraint(weight, pltpu.HBM))
 
 
-def early(blocks, first, weight, n_dev, per_dev):
+def early(blocks, first, weight, n_dev, span, per_dev):
     width = weight.shape[0]
     rows = len(blocks) * height(blocks[0], width)
     rest = weight.shape[1] - first.shape[1]
     return call(
-        functools.partial(early_kernel, len(blocks), per_dev),
+        functools.partial(early_kernel, len(blocks), span, per_dev),
         "early",
         (*blocks, first, weight),
         (VMEM,) * (len(blocks) + 1) + (pltpu.HBM,),
@@ -285,11 +303,11 @@
     )
 
 
-def late(blocks, held, before, n_dev, per_dev):
+def late(blocks, held, before, n_dev, span, per_dev):
     width = held[0].shape[0]
     rows = len(blocks) * height(blocks[0], width)
     return call(
-        functools.partial(late_kernel, len(blocks), per_dev),
+        functools.partial(late_kernel, len(blocks), span, per_dev),
         "late",
         (*blocks, *held, before),
         (VMEM,) * (len(blocks) + 2) + (None,),
@@ -356,10 +374,10 @@
     left, below = lax.optimization_barrier((left, below))
     far = [shift(below, -1, y, n_voc) for y in range(n_voc // RING)]
     corners = [shift(a, 0, y, n_voc) for y in over_y for a in (below, above)]
-    sent, right = early([own, below, *beside, above][:MOST], left, head_weight, n_dev, per_dev)
+    sent, right = early([own, below, *beside, above][:MOST], left, head_weight, n_dev, span, per_dev)
     rest = [own, below, *beside, above][MOST:] + [*corners, *far]
     for at in range(0, len(rest), MOST):
-        sent = late(rest[at : at + MOST], (left, right), sent, n_dev, per_dev)
+        sent = late(rest[at : at + MOST], (left, right), sent, n_dev, span, per_dev)
     everything = lax.all_to_all(sent, ("tok", "voc"), 0, 0, tiled=True)
     return finish(everything, req_dev, span)
 

time: 47.6 us -> 47.3 us (level)
  Pallas kernels: 22.2 us -> 21.3 us
  blocking collectives: 10.9 us -> 11.4 us
    pallas_call x2, Pallas kernels: 16 us -> 15.2 us  [call(): pl.pallas_call(kernel, out_shape=out_shape, in_specs=specs, out_specs=jax...]
    all_to_all x1, blocking collectives: 10.9 us -> 11.4 us  [shards(): everything = lax.all_to_all(sent, ('tok', 'voc'), 0, 0, tiled=True)]
  transfers between devices with their start and end apart: 7 -> 7, of which waited for: 0 -> 0; matrix products, arithmetic and copies ran while one was open for 0% -> 0% of each run, Pallas kernels for 27% -> 26%
where the time goes in v5:
time: 47.3 us; the launch traced here: 47.1 us
  Pallas kernels  21.3 us (45%)
  starting transfers between devices  13.7 us (29%)
  blocking collectives  11.4 us (24%)
  between operations  0.7 us (1%)
    pallas_call x2, Pallas kernels, call(): pl.pallas_call(kernel, out_shape=out_shape, in_specs=specs, out_specs=jax...  15.2 us
    ppermute x7, starting transfers between devices, shift(): return lax.ppermute(block, 'voc', pairs)  13.7 us
    all_to_all x1, blocking collectives, shards(): everything = lax.all_to_all(sent, ('tok', 'voc'), 0, 0, tiled=True)  11.4 us
    pallas_call x1, Pallas kernels, preload(): pl.pallas_call(preload_kernel, out_shape=VMEM((weight.shape[0], cut), BF1...  4.09 us
    pallas_call x1, Pallas kernels, pack(): pl.pallas_call(functools.partial(pack_kernel, n_voc), out_shape=jax.Shape...  1.34 us
  transfers between devices with their start and end apart: 7, of which 0 were waited for; matrix products, arithmetic and copies ran while one was open for 0% of the time, Pallas kernels for 26%

profile of v5, /device:TPU:0, one launch (start us, length us, event | category | flops | bytes accessed | tf_op | source)
XLA Modules:
  0.0 47.1 jit_solution(16962454396384864381)
XLA Ops:
  0.6 1.3 %pack.1.after_ref.refs_0_ = bf16[784,128]{1,0:T(8,128)(2,1)S(1)} custom-call(s32[2]{0:T(128)} %refs_0_.1, s32[2]{0:T(128)} %refs_1_.1, s32[64]{0:T(128)} %refs_2_.1, bf16[2,32,2048]{2,1,0:T(8,128)(2,1)} %refs_3_.1, f32[1,2048]{1,0:T(1,128)} %bitcast.1, s32[2,32]{1,0:T(2,128)} %refs_5_.2), custom_call_target="tpu_custom_call" | custom-call | tf_op jit(solution)/shard_map/pack/pallas_call | solution.py:83
  2.0 5.1 %collective-permute-start = (bf16[784,128]{1,0:T(8,128)(2,1)S(1)}, bf16[784,128]{1,0:T(8,128)(2,1)S(1)}, u32[]{:S(2)}, u32[]{:S(2)}) collective-permute-start(bf16[784,128]{1,0:T(8,128)(2,1)S(1)} %pack.1.after_ref.refs_0_), channel_id=1, source_target_pairs={{0,6},{1,7},{2,0},{3,1},{4,2},{5,3},{6,4},{7,5},{8,14},{9,15},{10,... | collective-permute-start | bytes 602120 | tf_op jit(solution)/shard_map/ppermute | solution.py:362
  7.1 0.0 collective-permute-start.2
  7.1 1.5 %collective-permute-start.6 = (bf16[784,128]{1,0:T(8,128)(2,1)S(1)}, bf16[784,128]{1,0:T(8,128)(2,1)S(1)}, u32[]{:S(2)}, u32[]{:S(2)}) collective-permute-start(bf16[784,128]{1,0:T(8,128)(2,1)S(1)} %pack.1.after_ref.refs_0_), channel_id=1, source_target_pairs={{0,1},{1,0},{2,3},{3,2},{4,5},{5,4},{6,7},{7,6},{8,9},{9,8},{10,11... | collective-permute-start | bytes 602120 | tf_op jit(solution)/shard_map/ppermute | solution.py:362
  8.6 4.1 %preload.1.refs_4_ = bf16[2048,2560]{1,0:T(8,128)(2,1)S(1)} custom-call(bf16[784,128]{1,0:T(8,128)(2,1)S(1)} %pack.1.after_ref.refs_0_, bf16[2048,6400]{1,0:T(8,128)(2,1)} %refs_5_.3), custom_call_target="tpu_custom_call" | custom-call | tf_op jit(solution)/shard_map/preload/pallas_call | solution.py:278
  12.7 0.0 collective-permute-done.refs_1_
  12.7 1.3 %collective-permute-start.1 = (bf16[784,128]{1,0:T(8,128)(2,1)S(1)}, bf16[784,128]{1,0:T(8,128)(2,1)S(1)}, u32[]{:S(2)}, u32[]{:S(2)}) collective-permute-start(bf16[784,128]{1,0:T(8,128)(2,1)S(1)} %collective-permute-done.refs_1_), channel_id=1, source_target_pairs={{0,1},{1,0},{2,3},{3,2},{4,5},{5,4},{6,7},{7,6},{8,9},{9,8},{10,11... | collective-permute-start | bytes 602120 | tf_op jit(solution)/shard_map/ppermute | solution.py:362
  14.0 4.3 %collective-permute-start.4 = (bf16[784,128]{1,0:T(8,128)(2,1)S(1)}, bf16[784,128]{1,0:T(8,128)(2,1)S(1)}, u32[]{:S(2)}, u32[]{:S(2)}) collective-permute-start(bf16[784,128]{1,0:T(8,128)(2,1)S(1)} %collective-permute-done.refs_1_), channel_id=1, source_target_pairs={{0,6},{1,7},{2,0},{3,1},{4,2},{5,3},{6,4},{7,5},{8,14},{9,15},{10,... | collective-permute-start | bytes 602120 | tf_op jit(solution)/shard_map/ppermute | solution.py:362
  18.3 0.0 collective-permute-start.5
  18.3 0.0 collective-permute-done.2.refs_3_
  18.3 1.5 %collective-permute-start.3 = (bf16[784,128]{1,0:T(8,128)(2,1)S(1)}, bf16[784,128]{1,0:T(8,128)(2,1)S(1)}, u32[]{:S(2)}, u32[]{:S(2)}) collective-permute-start(bf16[784,128]{1,0:T(8,128)(2,1)S(1)} %collective-permute-done.2.refs_3_), channel_id=1, source_target_pairs={{0,1},{1,0},{2,3},{3,2},{4,5},{5,4},{6,7},{7,6},{8,9},{9,8},{10,11... | collective-permute-start | bytes 602120 | tf_op jit(solution)/shard_map/ppermute | solution.py:362
  19.8 0.0 collective-permute-done.6.refs_2_
  19.8 8.4 %early.1 = (f32[32,4,128]{2,1,0:T(4,128)S(1)}, bf16[2048,3840]{1,0:T(8,128)(2,1)S(1)}) custom-call(bf16[784,128]{1,0:T(8,128)(2,1)S(1)} %pack.1.after_ref.refs_0_, bf16[784,128]{1,0:T(8,128)(2,1)S(1)} %collective-permute-done.refs_1_, bf16[784,128]{1,0:T(8,128)(2,1)S(1)} %collective-permute-done.6.refs_2_, ...), custom_call_target="tpu_custom_call" | custom-call | flops 5033164800 | bytes 26214400 | tf_op jit(solution)/shard_map/early/pallas_call | solution.py:263
  28.1 0.0 collective-permute-done.1.refs_0_
  28.1 0.0 collective-permute-done.4.refs_2_
  28.1 0.0 collective-permute-done.5.refs_3_
  28.2 0.0 collective-permute-done.3.refs_1_
  28.2 6.8 %late.1 = f32[32,4,128]{2,1,0:T(4,128)S(1)} custom-call(bf16[784,128]{1,0:T(8,128)(2,1)S(1)} %collective-permute-done.1.refs_0_, bf16[784,128]{1,0:T(8,128)(2,1)S(1)} %collective-permute-done.3.refs_1_, bf16[784,128]{1,0:T(8,128)(2,1)S(1)} %collective-permute-done.4.refs_2_, bf16[784,128]{1,0:T(8,128)(2,1)S(1)} %collective-permute-done.5.refs_3_, ...), custom_call_target="tpu_custom_call" | custom-call | flops 5033164800 | bytes 26214400 | tf_op jit(solution)/shard_map/late/pallas_call | solution.py:263
  35.0 11.4 %all_to_all.5.all_ref = f32[32,4,128]{2,1,0:T(4,128)S(1)} all-to-all(f32[32,4,128]{2,1,0:T(4,128)S(1)} %late.1), channel_id=1, replica_groups=mesh['tok'=4,'voc'=8] {'tok','voc'}, dimensions={0} | all-to-all | bytes 131072 | tf_op jit(solution)/shard_map/all_to_all | solution.py:381
  46.4 0.7 %finish.1 = (f32[2,32]{1,0:T(2,128)}, f32[2,32]{1,0:T(2,128)}) custom-call(f32[32,4,128]{2,1,0:T(4,128)S(1)} %all_to_all.5.all_ref), custom_call_target="tpu_custom_call" | custom-call | tf_op jit(solution)/shard_map/finish/pallas_call | solution.py:345
Async XLA Ops:
  2.0 10.7 %collective-permute-start = (bf16[784,128]{1,0:T(8,128)(2,1)S(1)}, bf16[784,128]{1,0:T(8,128)(2,1)S(1)}, u32[]{:S(2)}, u32[]{:S(2)}) collective-permute-start(bf16[784,128]{1,0:T(8,128)(2,1)S(1)} %pack.1.after_ref.refs_0_), channel_id=1, source_target_pairs={{0,6},{1,7},{2,0},{3,1},{4,2},{5,3},{6,4},{7,5},{8,14},{9,15},{10,... | collective-permute-start | bytes 602120 | tf_op jit(solution)/shard_map/ppermute | solution.py:362
  7.1 11.2 %collective-permute-start.2 = (bf16[784,128]{1,0:T(8,128)(2,1)S(1)}, bf16[784,128]{1,0:T(8,128)(2,1)S(1)}, u32[]{:S(2)}, u32[]{:S(2)}) collective-permute-start(bf16[784,128]{1,0:T(8,128)(2,1)S(1)} %pack.1.after_ref.refs_0_), channel_id=1, source_target_pairs={{0,2},{1,3},{2,4},{3,5},{4,6},{5,7},{6,0},{7,1},{8,10},{9,11},{10,... | collective-permute-start | bytes 602120 | tf_op jit(solution)/shard_map/ppermute | solution.py:362
  7.1 12.7 %collective-permute-start.6 = (bf16[784,128]{1,0:T(8,128)(2,1)S(1)}, bf16[784,128]{1,0:T(8,128)(2,1)S(1)}, u32[]{:S(2)}, u32[]{:S(2)}) collective-permute-start(bf16[784,128]{1,0:T(8,128)(2,1)S(1)} %pack.1.after_ref.refs_0_), channel_id=1, source_target_pairs={{0,1},{1,0},{2,3},{3,2},{4,5},{5,4},{6,7},{7,6},{8,9},{9,8},{10,11... | collective-permute-start | bytes 602120 | tf_op jit(solution)/shard_map/ppermute | solution.py:362
  12.7 15.4 %collective-permute-start.1 = (bf16[784,128]{1,0:T(8,128)(2,1)S(1)}, bf16[784,128]{1,0:T(8,128)(2,1)S(1)}, u32[]{:S(2)}, u32[]{:S(2)}) collective-permute-start(bf16[784,128]{1,0:T(8,128)(2,1)S(1)} %collective-permute-done.refs_1_), channel_id=1, source_target_pairs={{0,1},{1,0},{2,3},{3,2},{4,5},{5,4},{6,7},{7,6},{8,9},{9,8},{10,11... | collective-permute-start | bytes 602120 | tf_op jit(solution)/shard_map/ppermute | solution.py:362
  14.0 14.1 %collective-permute-start.4 = (bf16[784,128]{1,0:T(8,128)(2,1)S(1)}, bf16[784,128]{1,0:T(8,128)(2,1)S(1)}, u32[]{:S(2)}, u32[]{:S(2)}) collective-permute-start(bf16[784,128]{1,0:T(8,128)(2,1)S(1)} %collective-permute-done.refs_1_), channel_id=1, source_target_pairs={{0,6},{1,7},{2,0},{3,1},{4,2},{5,3},{6,4},{7,5},{8,14},{9,15},{10,... | collective-permute-start | bytes 602120 | tf_op jit(solution)/shard_map/ppermute | solution.py:362
  18.3 9.9 %collective-permute-start.5 = (bf16[784,128]{1,0:T(8,128)(2,1)S(1)}, bf16[784,128]{1,0:T(8,128)(2,1)S(1)}, u32[]{:S(2)}, u32[]{:S(2)}) collective-permute-start(bf16[784,128]{1,0:T(8,128)(2,1)S(1)} %collective-permute-done.refs_1_), channel_id=1, source_target_pairs={{0,7},{1,6},{2,1},{3,0},{4,3},{5,2},{6,5},{7,4},{8,15},{9,14},{10,... | collective-permute-start | bytes 602120 | tf_op jit(solution)/shard_map/ppermute | solution.py:362
  18.3 9.9 %collective-permute-start.3 = (bf16[784,128]{1,0:T(8,128)(2,1)S(1)}, bf16[784,128]{1,0:T(8,128)(2,1)S(1)}, u32[]{:S(2)}, u32[]{:S(2)}) collective-permute-start(bf16[784,128]{1,0:T(8,128)(2,1)S(1)} %collective-permute-done.2.refs_3_), channel_id=1, source_target_pairs={{0,1},{1,0},{2,3},{3,2},{4,5},{5,4},{6,7},{7,6},{8,9},{9,8},{10,11... | collective-permute-start | bytes 602120 | tf_op jit(solution)/shard_map/ppermute | solution.py:362

commit v6 on v5

--- a/solution.py
+++ b/solution.py
@@ -367,12 +367,12 @@
     n_dev, per_dev = n_tok * n_voc, req_dev * span
     over_y = range(1, n_voc // RING)
     own = pack(hidden, norm_gain, lengths, offsets, slot_request, targets, n_voc)
-    below = shift(own, -1, 0, n_voc)
+    below = shift(own, 1, 0, n_voc)
     beside = [shift(own, 0, y, n_voc) for y in over_y]
-    above = shift(own, 1, 0, n_voc)
+    above = shift(own, -1, 0, n_voc)
     left = preload(own, head_weight, CUT)
-    left, below = lax.optimization_barrier((left, below))
-    far = [shift(below, -1, y, n_voc) for y in range(n_voc // RING)]
+    left, below, beside = lax.optimization_barrier((left, below, beside))
+    far = [shift(below, 1, y, n_voc) for y in range(n_voc // RING)]
     corners = [shift(a, 0, y, n_voc) for y in over_y for a in (below, above)]
     sent, right = early([own, below, *beside, above][:MOST], left, head_weight, n_dev, span, per_dev)
     rest = [own, below, *beside, above][MOST:] + [*corners, *far]

time: 47.3 us -> 47.3 us (level)
  no operation moved by 1% of the time
where the time goes in v6:
time: 47.3 us; the launch traced here: 47.1 us
  Pallas kernels  21.3 us (45%)
  starting transfers between devices  13.8 us (29%)
  blocking collectives  11.3 us (24%)
  between operations  0.7 us (1%)
    pallas_call x2, Pallas kernels, call(): pl.pallas_call(kernel, out_shape=out_shape, in_specs=specs, out_specs=jax...  15.2 us
    ppermute x7, starting transfers between devices, shift(): return lax.ppermute(block, 'voc', pairs)  13.8 us
    all_to_all x1, blocking collectives, shards(): everything = lax.all_to_all(sent, ('tok', 'voc'), 0, 0, tiled=True)  11.3 us
    pallas_call x1, Pallas kernels, preload(): pl.pallas_call(preload_kernel, out_shape=VMEM((weight.shape[0], cut), BF1...  4.09 us
    pallas_call x1, Pallas kernels, pack(): pl.pallas_call(functools.partial(pack_kernel, n_voc), out_shape=jax.Shape...  1.34 us
  transfers between devices with their start and end apart: 7, of which 0 were waited for; matrix products, arithmetic and copies ran while one was open for 0% of the time, Pallas kernels for 26%

profile of v6, /device:TPU:0, one launch (start us, length us, event | category | flops | bytes accessed | tf_op | source)
XLA Modules:
  0.0 47.1 jit_solution(1369067477595376689)
XLA Ops:
  0.6 1.3 %pack.1.after_ref.refs_0_ = bf16[784,128]{1,0:T(8,128)(2,1)S(1)} custom-call(s32[2]{0:T(128)} %refs_0_.1, s32[2]{0:T(128)} %refs_1_.1, s32[64]{0:T(128)} %refs_2_.1, bf16[2,32,2048]{2,1,0:T(8,128)(2,1)} %refs_3_.1, f32[1,2048]{1,0:T(1,128)} %bitcast.1, s32[2,32]{1,0:T(2,128)} %refs_5_.2), custom_call_target="tpu_custom_call" | custom-call | tf_op jit(solution)/shard_map/pack/pallas_call | solution.py:83
  2.0 3.1 %collective-permute-start = (bf16[784,128]{1,0:T(8,128)(2,1)S(1)}, bf16[784,128]{1,0:T(8,128)(2,1)S(1)}, u32[]{:S(2)}, u32[]{:S(2)}) collective-permute-start(bf16[784,128]{1,0:T(8,128)(2,1)S(1)} %pack.1.after_ref.refs_0_), channel_id=1, source_target_pairs={{0,2},{1,3},{2,4},{3,5},{4,6},{5,7},{6,0},{7,1},{8,10},{9,11},{10,... | collective-permute-start | bytes 602120 | tf_op jit(solution)/shard_map/ppermute | solution.py:362
  5.1 1.5 %collective-permute-start.1 = (bf16[784,128]{1,0:T(8,128)(2,1)S(1)}, bf16[784,128]{1,0:T(8,128)(2,1)S(1)}, u32[]{:S(2)}, u32[]{:S(2)}) collective-permute-start(bf16[784,128]{1,0:T(8,128)(2,1)S(1)} %pack.1.after_ref.refs_0_), channel_id=1, source_target_pairs={{0,1},{1,0},{2,3},{3,2},{4,5},{5,4},{6,7},{7,6},{8,9},{9,8},{10,11... | collective-permute-start | bytes 602120 | tf_op jit(solution)/shard_map/ppermute | solution.py:362
  6.6 2.2 %collective-permute-start.3 = (bf16[784,128]{1,0:T(8,128)(2,1)S(1)}, bf16[784,128]{1,0:T(8,128)(2,1)S(1)}, u32[]{:S(2)}, u32[]{:S(2)}) collective-permute-start(bf16[784,128]{1,0:T(8,128)(2,1)S(1)} %pack.1.after_ref.refs_0_), channel_id=1, source_target_pairs={{0,6},{1,7},{2,0},{3,1},{4,2},{5,3},{6,4},{7,5},{8,14},{9,15},{10,... | collective-permute-start | bytes 602120 | tf_op jit(solution)/shard_map/ppermute | solution.py:362
  8.8 4.1 %preload.1.refs_4_ = bf16[2048,2560]{1,0:T(8,128)(2,1)S(1)} custom-call(bf16[784,128]{1,0:T(8,128)(2,1)S(1)} %pack.1.after_ref.refs_0_, bf16[2048,6400]{1,0:T(8,128)(2,1)} %refs_5_.3), custom_call_target="tpu_custom_call" | custom-call | tf_op jit(solution)/shard_map/preload/pallas_call | solution.py:278
  12.9 0.0 collective-permute-done.refs_1_
  12.9 0.0 collective-permute-done.1.refs_2_
  12.9 1.8 %collective-permute-start.2 = (bf16[784,128]{1,0:T(8,128)(2,1)S(1)}, bf16[784,128]{1,0:T(8,128)(2,1)S(1)}, u32[]{:S(2)}, u32[]{:S(2)}) collective-permute-start(bf16[784,128]{1,0:T(8,128)(2,1)S(1)} %collective-permute-done.refs_1_), channel_id=1, source_target_pairs={{0,1},{1,0},{2,3},{3,2},{4,5},{5,4},{6,7},{7,6},{8,9},{9,8},{10,11... | collective-permute-start | bytes 602120 | tf_op jit(solution)/shard_map/ppermute | solution.py:362
  14.7 0.0 collective-permute-start.5
  14.7 4.0 %collective-permute-start.6 = (bf16[784,128]{1,0:T(8,128)(2,1)S(1)}, bf16[784,128]{1,0:T(8,128)(2,1)S(1)}, u32[]{:S(2)}, u32[]{:S(2)}) collective-permute-start(bf16[784,128]{1,0:T(8,128)(2,1)S(1)} %collective-permute-done.refs_1_), channel_id=1, source_target_pairs={{0,3},{1,2},{2,5},{3,4},{4,7},{5,6},{6,1},{7,0},{8,11},{9,10},{10,... | collective-permute-start | bytes 602120 | tf_op jit(solution)/shard_map/ppermute | solution.py:362
  18.7 0.0 collective-permute-done.3.refs_3_
  18.7 1.2 %collective-permute-start.4 = (bf16[784,128]{1,0:T(8,128)(2,1)S(1)}, bf16[784,128]{1,0:T(8,128)(2,1)S(1)}, u32[]{:S(2)}, u32[]{:S(2)}) collective-permute-start(bf16[784,128]{1,0:T(8,128)(2,1)S(1)} %collective-permute-done.3.refs_3_), channel_id=1, source_target_pairs={{0,1},{1,0},{2,3},{3,2},{4,5},{5,4},{6,7},{7,6},{8,9},{9,8},{10,11... | collective-permute-start | bytes 602120 | tf_op jit(solution)/shard_map/ppermute | solution.py:362
  19.9 8.4 %early.1 = (f32[32,4,128]{2,1,0:T(4,128)S(1)}, bf16[2048,3840]{1,0:T(8,128)(2,1)S(1)}) custom-call(bf16[784,128]{1,0:T(8,128)(2,1)S(1)} %pack.1.after_ref.refs_0_, bf16[784,128]{1,0:T(8,128)(2,1)S(1)} %collective-permute-done.refs_1_, bf16[784,128]{1,0:T(8,128)(2,1)S(1)} %collective-permute-done.1.refs_2_, ...), custom_call_target="tpu_custom_call" | custom-call | flops 5033164800 | bytes 26214400 | tf_op jit(solution)/shard_map/early/pallas_call | solution.py:263
  28.2 0.0 collective-permute-done.2.refs_0_
  28.3 0.0 collective-permute-done.5.refs_2_
  28.3 0.0 collective-permute-done.6.refs_3_
  28.3 0.0 collective-permute-done.4.refs_1_
  28.3 6.8 %late.1 = f32[32,4,128]{2,1,0:T(4,128)S(1)} custom-call(bf16[784,128]{1,0:T(8,128)(2,1)S(1)} %collective-permute-done.2.refs_0_, bf16[784,128]{1,0:T(8,128)(2,1)S(1)} %collective-permute-done.4.refs_1_, bf16[784,128]{1,0:T(8,128)(2,1)S(1)} %collective-permute-done.5.refs_2_, bf16[784,128]{1,0:T(8,128)(2,1)S(1)} %collective-permute-done.6.refs_3_, ...), custom_call_target="tpu_custom_call" | custom-call | flops 5033164800 | bytes 26214400 | tf_op jit(solution)/shard_map/late/pallas_call | solution.py:263
  35.1 11.3 %all_to_all.5.all_ref = f32[32,4,128]{2,1,0:T(4,128)S(1)} all-to-all(f32[32,4,128]{2,1,0:T(4,128)S(1)} %late.1), channel_id=1, replica_groups=mesh['tok'=4,'voc'=8] {'tok','voc'}, dimensions={0} | all-to-all | bytes 131072 | tf_op jit(solution)/shard_map/all_to_all | solution.py:381
  46.4 0.7 %finish.1 = (f32[2,32]{1,0:T(2,128)}, f32[2,32]{1,0:T(2,128)}) custom-call(f32[32,4,128]{2,1,0:T(4,128)S(1)} %all_to_all.5.all_ref), custom_call_target="tpu_custom_call" | custom-call | tf_op jit(solution)/shard_map/finish/pallas_call | solution.py:345
Async XLA Ops:
  2.0 11.0 %collective-permute-start = (bf16[784,128]{1,0:T(8,128)(2,1)S(1)}, bf16[784,128]{1,0:T(8,128)(2,1)S(1)}, u32[]{:S(2)}, u32[]{:S(2)}) collective-permute-start(bf16[784,128]{1,0:T(8,128)(2,1)S(1)} %pack.1.after_ref.refs_0_), channel_id=1, source_target_pairs={{0,2},{1,3},{2,4},{3,5},{4,6},{5,7},{6,0},{7,1},{8,10},{9,11},{10,... | collective-permute-start | bytes 602120 | tf_op jit(solution)/shard_map/ppermute | solution.py:362
  5.1 7.9 %collective-permute-start.1 = (bf16[784,128]{1,0:T(8,128)(2,1)S(1)}, bf16[784,128]{1,0:T(8,128)(2,1)S(1)}, u32[]{:S(2)}, u32[]{:S(2)}) collective-permute-start(bf16[784,128]{1,0:T(8,128)(2,1)S(1)} %pack.1.after_ref.refs_0_), channel_id=1, source_target_pairs={{0,1},{1,0},{2,3},{3,2},{4,5},{5,4},{6,7},{7,6},{8,9},{9,8},{10,11... | collective-permute-start | bytes 602120 | tf_op jit(solution)/shard_map/ppermute | solution.py:362
  6.6 12.1 %collective-permute-start.3 = (bf16[784,128]{1,0:T(8,128)(2,1)S(1)}, bf16[784,128]{1,0:T(8,128)(2,1)S(1)}, u32[]{:S(2)}, u32[]{:S(2)}) collective-permute-start(bf16[784,128]{1,0:T(8,128)(2,1)S(1)} %pack.1.after_ref.refs_0_), channel_id=1, source_target_pairs={{0,6},{1,7},{2,0},{3,1},{4,2},{5,3},{6,4},{7,5},{8,14},{9,15},{10,... | collective-permute-start | bytes 602120 | tf_op jit(solution)/shard_map/ppermute | solution.py:362
  12.9 15.3 %collective-permute-start.2 = (bf16[784,128]{1,0:T(8,128)(2,1)S(1)}, bf16[784,128]{1,0:T(8,128)(2,1)S(1)}, u32[]{:S(2)}, u32[]{:S(2)}) collective-permute-start(bf16[784,128]{1,0:T(8,128)(2,1)S(1)} %collective-permute-done.refs_1_), channel_id=1, source_target_pairs={{0,1},{1,0},{2,3},{3,2},{4,5},{5,4},{6,7},{7,6},{8,9},{9,8},{10,11... | collective-permute-start | bytes 602120 | tf_op jit(solution)/shard_map/ppermute | solution.py:362
  14.7 13.5 %collective-permute-start.5 = (bf16[784,128]{1,0:T(8,128)(2,1)S(1)}, bf16[784,128]{1,0:T(8,128)(2,1)S(1)}, u32[]{:S(2)}, u32[]{:S(2)}) collective-permute-start(bf16[784,128]{1,0:T(8,128)(2,1)S(1)} %collective-permute-done.refs_1_), channel_id=1, source_target_pairs={{0,2},{1,3},{2,4},{3,5},{4,6},{5,7},{6,0},{7,1},{8,10},{9,11},{10,... | collective-permute-start | bytes 602120 | tf_op jit(solution)/shard_map/ppermute | solution.py:362
  14.7 13.5 %collective-permute-start.6 = (bf16[784,128]{1,0:T(8,128)(2,1)S(1)}, bf16[784,128]{1,0:T(8,128)(2,1)S(1)}, u32[]{:S(2)}, u32[]{:S(2)}) collective-permute-start(bf16[784,128]{1,0:T(8,128)(2,1)S(1)} %collective-permute-done.refs_1_), channel_id=1, source_target_pairs={{0,3},{1,2},{2,5},{3,4},{4,7},{5,6},{6,1},{7,0},{8,11},{9,10},{10,... | collective-permute-start | bytes 602120 | tf_op jit(solution)/shard_map/ppermute | solution.py:362
  18.7 9.6 %collective-permute-start.4 = (bf16[784,128]{1,0:T(8,128)(2,1)S(1)}, bf16[784,128]{1,0:T(8,128)(2,1)S(1)}, u32[]{:S(2)}, u32[]{:S(2)}) collective-permute-start(bf16[784,128]{1,0:T(8,128)(2,1)S(1)} %collective-permute-done.3.refs_3_), channel_id=1, source_target_pairs={{0,1},{1,0},{2,3},{3,2},{4,5},{5,4},{6,7},{7,6},{8,9},{9,8},{10,11... | collective-permute-start | bytes 602120 | tf_op jit(solution)/shard_map/ppermute | solution.py:362

commit v7 on v5

--- a/solution.py
+++ b/solution.py
@@ -16,7 +16,7 @@
 NOWHERE = (1 << (2 * DIGIT)) - 1
 STATS = 4
 TILE = 1280
-SHORT = 512
+SHORT = 256
 MOST = 4
 CUT = 2560
 PIECE = 1280

time: 47.3 us -> 47.3 us (level)
  no operation moved by 1% of the time
where the time goes in v7:
time: 47.3 us; the launch traced here: 47.1 us
  Pallas kernels  21.3 us (45%)
  starting transfers between devices  13.7 us (29%)
  blocking collectives  11.4 us (24%)
  between operations  0.7 us (1%)
    pallas_call x2, Pallas kernels, call(): pl.pallas_call(kernel, out_shape=out_shape, in_specs=specs, out_specs=jax...  15.2 us
    ppermute x7, starting transfers between devices, shift(): return lax.ppermute(block, 'voc', pairs)  13.7 us
    all_to_all x1, blocking collectives, shards(): everything = lax.all_to_all(sent, ('tok', 'voc'), 0, 0, tiled=True)  11.4 us
    pallas_call x1, Pallas kernels, preload(): pl.pallas_call(preload_kernel, out_shape=VMEM((weight.shape[0], cut), BF1...  4.09 us
    pallas_call x1, Pallas kernels, pack(): pl.pallas_call(functools.partial(pack_kernel, n_voc), out_shape=jax.Shape...  1.34 us
  transfers between devices with their start and end apart: 7, of which 0 were waited for; matrix products, arithmetic and copies ran while one was open for 0% of the time, Pallas kernels for 26%

profile of v7, /device:TPU:0, one launch (start us, length us, event | category | flops | bytes accessed | tf_op | source)
XLA Modules:
  0.0 47.1 jit_solution(15500885591747053296)
XLA Ops:
  0.6 1.3 %pack.1.after_ref.refs_0_ = bf16[784,128]{1,0:T(8,128)(2,1)S(1)} custom-call(s32[2]{0:T(128)} %refs_0_.1, s32[2]{0:T(128)} %refs_1_.1, s32[64]{0:T(128)} %refs_2_.1, bf16[2,32,2048]{2,1,0:T(8,128)(2,1)} %refs_3_.1, f32[1,2048]{1,0:T(1,128)} %bitcast.1, s32[2,32]{1,0:T(2,128)} %refs_5_.2), custom_call_target="tpu_custom_call" | custom-call | tf_op jit(solution)/shard_map/pack/pallas_call | solution.py:83
  2.0 5.1 %collective-permute-start = (bf16[784,128]{1,0:T(8,128)(2,1)S(1)}, bf16[784,128]{1,0:T(8,128)(2,1)S(1)}, u32[]{:S(2)}, u32[]{:S(2)}) collective-permute-start(bf16[784,128]{1,0:T(8,128)(2,1)S(1)} %pack.1.after_ref.refs_0_), channel_id=1, source_target_pairs={{0,6},{1,7},{2,0},{3,1},{4,2},{5,3},{6,4},{7,5},{8,14},{9,15},{10,... | collective-permute-start | bytes 602120 | tf_op jit(solution)/shard_map/ppermute | solution.py:362
  7.1 0.0 collective-permute-start.2
  7.1 1.5 %collective-permute-start.6 = (bf16[784,128]{1,0:T(8,128)(2,1)S(1)}, bf16[784,128]{1,0:T(8,128)(2,1)S(1)}, u32[]{:S(2)}, u32[]{:S(2)}) collective-permute-start(bf16[784,128]{1,0:T(8,128)(2,1)S(1)} %pack.1.after_ref.refs_0_), channel_id=1, source_target_pairs={{0,1},{1,0},{2,3},{3,2},{4,5},{5,4},{6,7},{7,6},{8,9},{9,8},{10,11... | collective-permute-start | bytes 602120 | tf_op jit(solution)/shard_map/ppermute | solution.py:362
  8.6 4.1 %preload.1.refs_4_ = bf16[2048,2560]{1,0:T(8,128)(2,1)S(1)} custom-call(bf16[784,128]{1,0:T(8,128)(2,1)S(1)} %pack.1.after_ref.refs_0_, bf16[2048,6400]{1,0:T(8,128)(2,1)} %refs_5_.3), custom_call_target="tpu_custom_call" | custom-call | tf_op jit(solution)/shard_map/preload/pallas_call | solution.py:278
  12.7 0.0 collective-permute-done.refs_1_
  12.7 1.3 %collective-permute-start.1 = (bf16[784,128]{1,0:T(8,128)(2,1)S(1)}, bf16[784,128]{1,0:T(8,128)(2,1)S(1)}, u32[]{:S(2)}, u32[]{:S(2)}) collective-permute-start(bf16[784,128]{1,0:T(8,128)(2,1)S(1)} %collective-permute-done.refs_1_), channel_id=1, source_target_pairs={{0,1},{1,0},{2,3},{3,2},{4,5},{5,4},{6,7},{7,6},{8,9},{9,8},{10,11... | collective-permute-start | bytes 602120 | tf_op jit(solution)/shard_map/ppermute | solution.py:362
  14.0 4.3 %collective-permute-start.4 = (bf16[784,128]{1,0:T(8,128)(2,1)S(1)}, bf16[784,128]{1,0:T(8,128)(2,1)S(1)}, u32[]{:S(2)}, u32[]{:S(2)}) collective-permute-start(bf16[784,128]{1,0:T(8,128)(2,1)S(1)} %collective-permute-done.refs_1_), channel_id=1, source_target_pairs={{0,6},{1,7},{2,0},{3,1},{4,2},{5,3},{6,4},{7,5},{8,14},{9,15},{10,... | collective-permute-start | bytes 602120 | tf_op jit(solution)/shard_map/ppermute | solution.py:362
  18.3 0.0 collective-permute-start.5
  18.3 0.0 collective-permute-done.2.refs_3_
  18.3 1.5 %collective-permute-start.3 = (bf16[784,128]{1,0:T(8,128)(2,1)S(1)}, bf16[784,128]{1,0:T(8,128)(2,1)S(1)}, u32[]{:S(2)}, u32[]{:S(2)}) collective-permute-start(bf16[784,128]{1,0:T(8,128)(2,1)S(1)} %collective-permute-done.2.refs_3_), channel_id=1, source_target_pairs={{0,1},{1,0},{2,3},{3,2},{4,5},{5,4},{6,7},{7,6},{8,9},{9,8},{10,11... | collective-permute-start | bytes 602120 | tf_op jit(solution)/shard_map/ppermute | solution.py:362
  19.8 0.0 collective-permute-done.6.refs_2_
  19.8 8.4 %early.1 = (f32[32,4,128]{2,1,0:T(4,128)S(1)}, bf16[2048,3840]{1,0:T(8,128)(2,1)S(1)}) custom-call(bf16[784,128]{1,0:T(8,128)(2,1)S(1)} %pack.1.after_ref.refs_0_, bf16[784,128]{1,0:T(8,128)(2,1)S(1)} %collective-permute-done.refs_1_, bf16[784,128]{1,0:T(8,128)(2,1)S(1)} %collective-permute-done.6.refs_2_, ...), custom_call_target="tpu_custom_call" | custom-call | flops 5033164800 | bytes 26214400 | tf_op jit(solution)/shard_map/early/pallas_call | solution.py:263
  28.2 0.0 collective-permute-done.1.refs_0_
  28.2 0.0 collective-permute-done.4.refs_2_
  28.2 0.0 collective-permute-done.5.refs_3_
  28.2 0.0 collective-permute-done.3.refs_1_
  28.2 6.8 %late.1 = f32[32,4,128]{2,1,0:T(4,128)S(1)} custom-call(bf16[784,128]{1,0:T(8,128)(2,1)S(1)} %collective-permute-done.1.refs_0_, bf16[784,128]{1,0:T(8,128)(2,1)S(1)} %collective-permute-done.3.refs_1_, bf16[784,128]{1,0:T(8,128)(2,1)S(1)} %collective-permute-done.4.refs_2_, bf16[784,128]{1,0:T(8,128)(2,1)S(1)} %collective-permute-done.5.refs_3_, ...), custom_call_target="tpu_custom_call" | custom-call | flops 5033164800 | bytes 26214400 | tf_op jit(solution)/shard_map/late/pallas_call | solution.py:263
  35.0 11.4 %all_to_all.5.all_ref = f32[32,4,128]{2,1,0:T(4,128)S(1)} all-to-all(f32[32,4,128]{2,1,0:T(4,128)S(1)} %late.1), channel_id=1, replica_groups=mesh['tok'=4,'voc'=8] {'tok','voc'}, dimensions={0} | all-to-all | bytes 131072 | tf_op jit(solution)/shard_map/all_to_all | solution.py:381
  46.4 0.7 %finish.1 = (f32[2,32]{1,0:T(2,128)}, f32[2,32]{1,0:T(2,128)}) custom-call(f32[32,4,128]{2,1,0:T(4,128)S(1)} %all_to_all.5.all_ref), custom_call_target="tpu_custom_call" | custom-call | tf_op jit(solution)/shard_map/finish/pallas_call | solution.py:345
Async XLA Ops:
  2.0 10.7 %collective-permute-start = (bf16[784,128]{1,0:T(8,128)(2,1)S(1)}, bf16[784,128]{1,0:T(8,128)(2,1)S(1)}, u32[]{:S(2)}, u32[]{:S(2)}) collective-permute-start(bf16[784,128]{1,0:T(8,128)(2,1)S(1)} %pack.1.after_ref.refs_0_), channel_id=1, source_target_pairs={{0,6},{1,7},{2,0},{3,1},{4,2},{5,3},{6,4},{7,5},{8,14},{9,15},{10,... | collective-permute-start | bytes 602120 | tf_op jit(solution)/shard_map/ppermute | solution.py:362
  7.1 11.2 %collective-permute-start.2 = (bf16[784,128]{1,0:T(8,128)(2,1)S(1)}, bf16[784,128]{1,0:T(8,128)(2,1)S(1)}, u32[]{:S(2)}, u32[]{:S(2)}) collective-permute-start(bf16[784,128]{1,0:T(8,128)(2,1)S(1)} %pack.1.after_ref.refs_0_), channel_id=1, source_target_pairs={{0,2},{1,3},{2,4},{3,5},{4,6},{5,7},{6,0},{7,1},{8,10},{9,11},{10,... | collective-permute-start | bytes 602120 | tf_op jit(solution)/shard_map/ppermute | solution.py:362
  7.1 12.7 %collective-permute-start.6 = (bf16[784,128]{1,0:T(8,128)(2,1)S(1)}, bf16[784,128]{1,0:T(8,128)(2,1)S(1)}, u32[]{:S(2)}, u32[]{:S(2)}) collective-permute-start(bf16[784,128]{1,0:T(8,128)(2,1)S(1)} %pack.1.after_ref.refs_0_), channel_id=1, source_target_pairs={{0,1},{1,0},{2,3},{3,2},{4,5},{5,4},{6,7},{7,6},{8,9},{9,8},{10,11... | collective-permute-start | bytes 602120 | tf_op jit(solution)/shard_map/ppermute | solution.py:362
  12.7 15.4 %collective-permute-start.1 = (bf16[784,128]{1,0:T(8,128)(2,1)S(1)}, bf16[784,128]{1,0:T(8,128)(2,1)S(1)}, u32[]{:S(2)}, u32[]{:S(2)}) collective-permute-start(bf16[784,128]{1,0:T(8,128)(2,1)S(1)} %collective-permute-done.refs_1_), channel_id=1, source_target_pairs={{0,1},{1,0},{2,3},{3,2},{4,5},{5,4},{6,7},{7,6},{8,9},{9,8},{10,11... | collective-permute-start | bytes 602120 | tf_op jit(solution)/shard_map/ppermute | solution.py:362
  14.0 14.2 %collective-permute-start.4 = (bf16[784,128]{1,0:T(8,128)(2,1)S(1)}, bf16[784,128]{1,0:T(8,128)(2,1)S(1)}, u32[]{:S(2)}, u32[]{:S(2)}) collective-permute-start(bf16[784,128]{1,0:T(8,128)(2,1)S(1)} %collective-permute-done.refs_1_), channel_id=1, source_target_pairs={{0,6},{1,7},{2,0},{3,1},{4,2},{5,3},{6,4},{7,5},{8,14},{9,15},{10,... | collective-permute-start | bytes 602120 | tf_op jit(solution)/shard_map/ppermute | solution.py:362
  18.3 9.9 %collective-permute-start.5 = (bf16[784,128]{1,0:T(8,128)(2,1)S(1)}, bf16[784,128]{1,0:T(8,128)(2,1)S(1)}, u32[]{:S(2)}, u32[]{:S(2)}) collective-permute-start(bf16[784,128]{1,0:T(8,128)(2,1)S(1)} %collective-permute-done.refs_1_), channel_id=1, source_target_pairs={{0,7},{1,6},{2,1},{3,0},{4,3},{5,2},{6,5},{7,4},{8,15},{9,14},{10,... | collective-permute-start | bytes 602120 | tf_op jit(solution)/shard_map/ppermute | solution.py:362
  18.3 9.9 %collective-permute-start.3 = (bf16[784,128]{1,0:T(8,128)(2,1)S(1)}, bf16[784,128]{1,0:T(8,128)(2,1)S(1)}, u32[]{:S(2)}, u32[]{:S(2)}) collective-permute-start(bf16[784,128]{1,0:T(8,128)(2,1)S(1)} %collective-permute-done.2.refs_3_), channel_id=1, source_target_pairs={{0,1},{1,0},{2,3},{3,2},{4,5},{5,4},{6,7},{7,6},{8,9},{9,8},{10,11... | collective-permute-start | bytes 602120 | tf_op jit(solution)/shard_map/ppermute | solution.py:362
